TPU v7x, 1024 devices: a whole 4x8x16 slice. The times are simulated.
1024 devices in a mesh: node: 64 (over x, z), local: 16 (over y, core).
Axes of the slice: x: 4, y: 8, z: 16, core: 2. Of those that a mesh axis runs over, the one named last changes fastest.
Arguments:
- tokens: bfloat16 [8192, 3584], P('node', 'local'), may hold values from -6 to 6
- cotangent: bfloat16 [8192, 3584], P('node', 'local'), may hold values from -6 to 6
- routes: int32 [8192, 8], P('node'), may hold values from 0 to 255, as said below
- gate_probs: bfloat16 [8192, 8], P('node'), may hold values from 0.049804688 to 0.5
- w_gate: bfloat16 [64, 3584, 2048], P('node', None, 'local'), may hold values from -0.09375 to 0.09375
- w_up: bfloat16 [64, 3584, 2048], P('node', None, 'local'), may hold values from -0.09375 to 0.09375
- w_down: bfloat16 [64, 2048, 3584], P('node', 'local'), may hold values from -0.125 to 0.125
- tile_noise: float32 [64, 3, 28, 2048], P('node', None, None, 'local'), may hold values from -0.5 to 0.5
Outputs:
- token_grad: bfloat16 [8192, 3584], P('node', 'local')
- probs_grad: bfloat16 [8192, 8], P('node')
- noise_grad: float32 [64, 3, 28, 2048], P('node', None, None, 'local')
Inputs may be any that keep to these rules, and one draw needn't show every extreme that they name: `routes`: each token names 8 different experts, two in each of 4 different groups, expert e lying in group e // 4. Among the 128 tokens of one index of node at most 2 name a given group's first expert (index a multiple of 4); in every draw one group's first expert is named by exactly 2 of them at every index of node.
All inputs are finite; a program needn't handle non-finite values.
Results may differ from a plain program's by a relative error of at most 0.029.
Values may be sent and summed in bfloat16 or wider, within the bound.
No kernel may reach another device: no remote copies, remote signals or barrier semaphores. Data moves between devices by JAX's collectives and lax.ppermute only.
A program may use at most 32 MiB of HBM per device.

v0:
```python
import math

import jax
import jax.numpy as jnp
from jax import lax
from jax.experimental import pallas as pl
from jax.experimental.pallas import tpu as pltpu
from jax.sharding import PartitionSpec as P

EXP_GROUP = 4
LANES = 128
TAIL = 16
FACTORS = 3
F32 = jnp.float32
F16 = jnp.float16
BF16 = jnp.bfloat16
ROWS_BY_ROWS = (((0,), (0,)), ((), ()))
LANES_BY_LANES = (((1,), (1,)), ((), ()))


def dot(a, b, dims=(((1,), (0,)), ((), ()))):
    return lax.dot_general(a, b, dims, preferred_element_type=F32)


def select_rows(routes_ref, per_group, copies, rows):
    top, tokens = routes_ref.shape
    row = lax.broadcasted_iota(jnp.int32, (rows, tokens), 0)
    first = lax.div(row, per_group) * EXP_GROUP
    slot = lax.rem(lax.div(row, copies), per_group // copies)
    matches = [routes_ref[j : j + 1, :] == first for j in range(top)]
    hit = jnp.zeros((rows, tokens), F32)
    for match in matches:
        hit = jnp.where(match, 1.0, hit)
    before = lax.broadcasted_iota(jnp.int32, (tokens, tokens), 0)
    after = lax.broadcasted_iota(jnp.int32, (tokens, tokens), 1)
    earlier = jnp.where(before < after, 1.0, 0.0).astype(BF16)
    rank = dot(hit.astype(BF16), earlier)
    chosen = jnp.where(rank == slot.astype(F32), hit, 0.0)
    return chosen, lax.rem(row, copies), matches


def pack_kernel(routes_ref, probs_ref, x_ref, dy_ref, out_ref):
    rows, lanes = out_ref.shape
    feats = x_ref.shape[0]
    chosen, block, matches = select_rows(routes_ref, 8, 4, rows)
    weight = jnp.zeros(chosen.shape, F32)
    for j, match in enumerate(matches):
        weight = jnp.where(match, probs_ref[j : j + 1, :].astype(F32), weight)
    weight = jnp.sum(weight * chosen, axis=1, keepdims=True)
    pad = jnp.zeros((4 * lanes - 2 * feats, lanes), BF16)
    both = jnp.concatenate([x_ref[...], dy_ref[...], pad], axis=0)
    picked = dot(chosen.astype(BF16), both, LANES_BY_LANES)
    out = jnp.zeros((rows, lanes), F32)
    for j in range(4):
        out = jnp.where(block == j, picked[:, j * lanes : (j + 1) * lanes], out)
    lane = lax.broadcasted_iota(jnp.int32, (rows, lanes), 1)
    out = jnp.where((block == 3) & (lane == 2 * feats - 3 * lanes), weight, out)
    out_ref[...] = out.astype(BF16)


def unpack_kernel(got_ref, xdy_ref, prob_ref):
    rows, lanes = got_ref.shape
    got = got_ref[...]
    row = lax.broadcasted_iota(jnp.int32, (rows, lanes), 0)
    col = lax.broadcasted_iota(jnp.int32, (rows, lanes), 1)
    parts = []
    for j in range(4):
        place = jnp.where(row == 4 * col + j, 1.0, 0.0).astype(BF16)
        parts.append(dot(got, place, ROWS_BY_ROWS))
    whole = jnp.concatenate(parts, axis=0)
    both = xdy_ref.shape[0] - TAIL
    feats = both // 2
    prob_ref[...] = whole[both : both + 8]
    undo = []
    for first in (0, feats):
        half = whole[first : first + feats]
        top = jnp.max(jnp.abs(half), axis=0, keepdims=True)
        raised = jnp.ones(top.shape, F32)
        for _ in range(FACTORS):
            factor = jnp.ones(top.shape, F32)
            for power in (256.0, 16.0, 4.0):
                fits = top * raised * power <= 32768.0
                raised = jnp.where(fits, raised * power, raised)
                factor = jnp.where(fits, factor / power, factor)
            undo.append(factor)
        xdy_ref[first : first + feats, :] = half * raised
    undo.append(jnp.ones((TAIL - 2 * FACTORS, lanes), F32))
    xdy_ref[both:, :] = jnp.concatenate(undo, axis=0)


def scale_kernel(
    after_ref, gate_ref, up_ref, down_ref, noise_ref, wide_ref, tall_ref, eff_down_ref, down_t_ref
):
    del after_ref
    blocks, lanes = noise_ref.shape[1:]
    for b in range(blocks):
        part = slice(b * lanes, (b + 1) * lanes)
        gate = gate_ref[part, :].astype(F32) * (1.0 + noise_ref[0, b : b + 1, :])
        up = up_ref[part, :].astype(F32) * (1.0 + noise_ref[1, b : b + 1, :])
        tall_ref[part, :lanes] = gate.astype(BF16)
        tall_ref[part, lanes:] = up.astype(BF16)
        wide_ref[:lanes, part] = gate.astype(BF16).T
        wide_ref[lanes:, part] = up.astype(BF16).T
        down = down_ref[:, part].T
        down_t_ref[part, :] = down
        back = down.astype(F32) * (1.0 + noise_ref[2, b : b + 1, :])
        eff_down_ref[:, part] = back.astype(BF16).T


def lower(rows_ref, x_ref, dy_ref):
    feats = (rows_ref.shape[1] - TAIL) // 2
    for i in range(rows_ref.shape[0]):
        for j, target in enumerate((x_ref, dy_ref)):
            first = 2 * feats + j * FACTORS
            undo = jnp.ones((1, rows_ref.shape[2]), F32)
            for k in range(FACTORS):
                undo = undo * rows_ref[i, first + k : first + k + 1, :].astype(F32)
            value = rows_ref[i, j * feats : (j + 1) * feats, :].astype(F32) * undo
            target[i * feats : (i + 1) * feats, :] = value.astype(BF16)


def main_kernel(
    core_ref, prob_ref, rows_hbm, wide_hbm, down_hbm, tall_hbm,
    keep_ref, send_ref, d_ref, rows_ref, wide_ref, down_ref, tall_ref, x_ref, dy_ref, sems,
):
    pairs = ((rows_hbm, rows_ref), (wide_hbm, wide_ref), (down_hbm, down_ref), (tall_hbm, tall_ref))
    moves = [
        pltpu.make_async_copy(source, target, sems.at[i])
        for i, (source, target) in enumerate(pairs)
    ]
    for move in moves:
        move.start()
    moves[0].wait()
    lower(rows_ref, x_ref, dy_ref)
    core = core_ref[0]
    hid = down_ref.shape[0]
    moves[1].wait()
    pre = dot(wide_ref[...], x_ref[...])
    moves[2].wait()
    back = dot(down_ref[...], dy_ref[...])
    pre_gate, pre_up = pre[:hid], pre[hid:]
    prob = prob_ref[0:1, :]
    sig = jax.nn.sigmoid(pre_gate)
    swish = pre_gate * sig
    hidden = (swish * pre_up).astype(BF16).astype(F32)
    grad_hidden = prob * back
    d_gate = grad_hidden * pre_up * sig * (1.0 + pre_gate * (1.0 - sig))
    d_up = grad_hidden * swish
    d_ref[:, :hid] = d_gate.T.astype(BF16)
    d_ref[:, hid : 2 * hid] = d_up.T.astype(BF16)
    d_ref[:, 2 * hid :] = (prob * hidden).T.astype(BF16)
    d_both = jnp.concatenate([d_gate.astype(BF16), d_up.astype(BF16)], axis=0)
    prob_term = jnp.sum(hidden * back, axis=0, keepdims=True)
    chips, rows, lanes = keep_ref.shape
    feats = x_ref.shape[0] // (2 * chips)
    line = lax.broadcasted_iota(jnp.int32, (rows - feats, lanes), 0)
    tail = jnp.where(line == 0, prob_term, 0.0).astype(BF16)
    moves[3].wait()
    for chip in range(chips):
        for target, rank in ((send_ref, 1 - core), (keep_ref, core)):
            start = pl.multiple_of((2 * chip + rank) * feats, 32)
            target[chip, :feats, :] = dot(tall_ref[pl.ds(start, feats), :], d_both).astype(BF16)
            target[chip, feats:, :] = tail


def noise_kernel(rows_ref, d_ref, gate_ref, up_ref, down_t_ref, out_ref, x_ref, dy_ref):
    lower(rows_ref, x_ref, dy_ref)
    blocks, lanes = out_ref.shape[1:]
    for b in range(blocks):
        part = slice(b * lanes, (b + 1) * lanes)
        grad = dot(x_ref[part, :], d_ref[:, : 2 * lanes])
        grad_down = dot(dy_ref[part, :], d_ref[:, 2 * lanes :])
        pieces = (
            (gate_ref, grad[:, :lanes]),
            (up_ref, grad[:, lanes:]),
            (down_t_ref, grad_down),
        )
        for i, (weight, value) in enumerate(pieces):
            out_ref[i, b : b + 1, :] = jnp.sum(
                weight[part, :].astype(F32) * value, axis=0, keepdims=True
            )


def collect_kernel(parts_ref, out_ref):
    rows, lanes = out_ref.shape
    chips, height, slots = parts_ref.shape
    total = parts_ref[0].astype(F32)
    for chip in range(1, chips):
        total = total + parts_ref[chip].astype(F32)
    pad = jnp.zeros((2 * lanes - height, slots), BF16)
    total = jnp.concatenate([total.astype(BF16), pad], axis=0)
    row = lax.broadcasted_iota(jnp.int32, (rows, slots), 0)
    col = lax.broadcasted_iota(jnp.int32, (rows, slots), 1)
    place = jnp.where(lax.div(row, 2) == col, 1.0, 0.0).astype(BF16)
    spread = dot(place, total, LANES_BY_LANES)
    odd = lax.rem(lax.broadcasted_iota(jnp.int32, (rows, lanes), 0), 2)
    out_ref[...] = jnp.where(odd == 0, spread[:, :lanes], spread[:, lanes:]).astype(BF16)


def finish_kernel(back_ref, routes_ref, tokens_ref, probs_ref):
    rows, lanes = back_ref.shape
    feats = tokens_ref.shape[0]
    chosen, block, matches = select_rows(routes_ref, 4, 2, rows)
    back = back_ref[...]
    low = dot(back, jnp.where(block == 0, chosen, 0.0).astype(BF16), ROWS_BY_ROWS)
    high_rows = jnp.where(block == 1, chosen, 0.0)
    high = dot(back, high_rows.astype(BF16), ROWS_BY_ROWS)
    tokens_ref[:lanes, :] = low.astype(BF16)
    tokens_ref[lanes:, :] = high[: feats - lanes].astype(BF16)
    given = back[:, feats - lanes : feats - lanes + 1].astype(F32) * high_rows
    lines = [
        jnp.sum(jnp.where(match, given, 0.0), axis=0, keepdims=True) for match in matches
    ]
    probs_ref[...] = jnp.concatenate(lines, axis=0).astype(BF16)


def call(kernel, outs, *args, scalars=0, scratch=(), limit=32, far=0):
    size = sum(math.prod(a.shape) * a.dtype.itemsize for a in [*args, *outs])
    specs = [pl.BlockSpec(memory_space=pltpu.SMEM)] * scalars
    specs += [pl.BlockSpec(memory_space=pltpu.VMEM)] * (len(args) - scalars - far)
    specs += [pl.BlockSpec(memory_space=pl.ANY)] * far
    return pl.pallas_call(
        kernel,
        out_shape=outs,
        in_specs=specs,
        out_specs=[pl.BlockSpec(memory_space=pltpu.VMEM)] * len(outs),
        scratch_shapes=list(scratch),
        compiler_params=pltpu.CompilerParams(vmem_limit_bytes=limit * 1024 * 1024),
        cost_estimate=pl.CostEstimate(flops=0, bytes_accessed=size, transcendentals=0),
    )(*args)


def shape(dims, dtype=BF16):
    return jax.ShapeDtypeStruct(dims, dtype)


def shards(tokens, cotangent, routes, gate_probs, w_gate, w_up, w_down, tile_noise):
    nodes = lax.axis_size("node")
    local = lax.axis_size("local")
    chips = local // 2
    count, feats = tokens.shape
    slots = 2 * nodes
    gate, up, down, noise = w_gate[0], w_up[0], w_down[0], tile_noise[0]
    width, hid = gate.shape
    routes_t = routes.T
    same_core = [[2 * y + c for y in range(chips)] for c in range(2)]
    swap = [(i, i ^ 1) for i in range(local)]
    core = lax.rem(lax.axis_index("local"), 2).astype(jnp.int32).reshape(1)

    (sent,) = call(
        pack_kernel,
        [shape((8 * nodes, LANES))],
        routes_t, gate_probs.T, tokens.T, cotangent.T,
        limit=60,
    )
    got = lax.all_to_all(sent.reshape(nodes, 8, LANES), "node", 0, 0, tiled=True)
    later, _ = lax.optimization_barrier((core, sent))
    scaled = call(
        scale_kernel,
        [
            pltpu.HBM((2 * hid, width), BF16),
            pltpu.HBM((width, 2 * hid), BF16),
            pltpu.HBM((hid, width), BF16),
            pltpu.HBM((width, hid), BF16),
        ],
        later, gate, up, down, noise,
        scalars=1,
    )
    got, scaled = lax.optimization_barrier((got, scaled))
    wide, tall, eff_down, down_t = scaled
    xdy, prob = call(
        unpack_kernel,
        [shape((2 * feats + TAIL, slots), F32), shape((8, slots), F32)],
        got.reshape(8 * nodes, LANES),
    )
    rows = lax.all_gather(xdy.astype(F16), "local", axis=0).astype(BF16)
    high = feats + 16
    keep, send, d_all = call(
        main_kernel,
        [
            pltpu.VMEM((chips, high, slots), BF16),
            pltpu.VMEM((chips, high, slots), BF16),
            pltpu.VMEM((slots, 3 * hid), BF16),
        ],
        core, prob, rows, wide, eff_down, tall,
        scalars=1,
        scratch=[
            pltpu.VMEM(rows.shape, BF16),
            pltpu.VMEM((2 * hid, width), BF16),
            pltpu.VMEM((hid, width), BF16),
            pltpu.VMEM((width, 2 * hid), BF16),
            pltpu.VMEM((width, slots), BF16),
            pltpu.VMEM((width, slots), BF16),
            pltpu.SemaphoreType.DMA((4,)),
        ],
        far=4,
        limit=57,
    )
    came = lax.ppermute(send, "local", swap)
    pair = (keep.astype(F32) + came.astype(F32)).astype(BF16)
    parts = lax.all_to_all(pair, "local", 0, 0, axis_index_groups=same_core, tiled=True)
    (noise_grad,) = call(
        noise_kernel,
        [shape(noise.shape, F32)],
        rows, d_all, gate, up, down_t,
        scratch=[pltpu.VMEM((width, slots), BF16), pltpu.VMEM((width, slots), BF16)],
    )
    (home,) = call(collect_kernel, [shape((4 * nodes, LANES))], parts)
    back = lax.all_to_all(home.reshape(nodes, 4, LANES), "node", 0, 0, tiled=True)
    token_t, probs_t = call(
        finish_kernel,
        [shape((feats, count)), shape((routes.shape[1], count))],
        back.reshape(4 * nodes, LANES),
        routes_t,
    )
    return token_t.T, probs_t.T, noise_grad[None]


def solution(mesh):
    in_specs = (
        P("node", "local"),
        P("node", "local"),
        P("node", None),
        P("node", None),
        P("node", None, "local"),
        P("node", None, "local"),
        P("node", "local", None),
        P("node", None, None, "local"),
    )
    out_specs = (P("node", "local"), P("node", None), P("node", None, None, "local"))
    return jax.shard_map(shards, mesh=mesh, in_specs=in_specs, out_specs=out_specs, check_vma=False)
```

profile of v0, /device:TPU:1, one launch (start us, length us, event | category | flops | bytes accessed | tf_op | source)
XLA Modules:
  0.0 119.3 jit_solution(15508991374374912417)
XLA Ops:
  0.6 2.2 %shard_map.103 = bf16[512,128]{1,0:T(8,128)(2,1)} custom-call(s32[8,128]{1,0:T(8,128)} %bitcast.30, bf16[8,128]{1,0:T(8,128)(2,1)} %bitcast.35, bf16[224,128]{1,0:T(8,128)(2,1)} %bitcast.33, bf16[224,128]{1,0:T(8,128)(2,1)} %bitcast.34), custom_call_target="tpu_custom_call" | custom-call | bytes 251904 | tf_op jit(solution)/shard_map/pallas_call | solution.py:222
  2.8 22.8 %all-to-all-start = ((bf16[64,8,128]{2,1,0:T(8,128)(2,1)}), bf16[64,8,128]{2,1,0:T(8,128)(2,1)S(1)}, u32[]{:S(2)}, u32[]{:S(2)}) async-start(bf16[64,8,128]{2,1,0:T(8,128)(2,1)} %bitcast.32), calls=%async_computation | async-start | bytes 262144 | tf_op jit(solution)/shard_map/all_to_all | solution.py:256
  25.6 0.8 copy.14
  26.4 1.2 copy-done.1
  27.6 1.2 copy-done.3
  28.8 1.2 copy-done.6
  30.0 3.3 %shard_map.104 = (bf16[256,3584]{1,0:T(8,128)(2,1)}, bf16[3584,256]{1,0:T(8,128)(2,1)}, bf16[128,3584]{1,0:T(8,128)(2,1)}, bf16[3584,128]{1,0:T(8,128)(2,1)}) custom-call(s32[1]{0:T(128)} %bitcast.after_ref.core_ref, bf16[3584,128]{1,0:T(8,128)(2,1)S(1)} %bitcast.21, bf16[3584,128]{1,0:T(8,128)(2,1)S(1)} %bitcast.23, bf16[128,3584]{1,0:T(8,128)(2,1)S(1)} %bitcast.25, ...), custom_call_target="tpu_custom_call" | custom-call | bytes 8300548 | tf_op jit(solution)/shard_map/pallas_call | solution.py:222
  33.3 6.3 %all-to-all-done = bf16[64,8,128]{2,1,0:T(8,128)(2,1)S(1)} async-done(((bf16[64,8,128]{2,1,0:T(8,128)(2,1)}), bf16[64,8,128]{2,1,0:T(8,128)(2,1)S(1)}, u32[]{:S(2)}, u32[]{:S(2)}) %all-to-all-start) | async-done | bytes 131104 | tf_op jit(solution)/shard_map/all_to_all | solution.py:256
  39.6 0.4 shard_map.105
  40.0 26.4 %all-gather.2 = f16[7424,128]{1,0:T(8,128)(2,1)S(1)} all-gather(f16[464,128]{1,0:T(8,128)(2,1)S(1)} %convert_element_type.15), channel_id=2, replica_groups=mesh['node'=64,'local'=16] {'local'}, dimensions={0}, use_global_device_ids=true | all-gather | bytes 2019328 | tf_op jit(solution)/shard_map/all_gather | solution.py:276
  66.4 1.5 %convert_element_type.20 = bf16[7424,128]{1,0:T(8,128)(2,1)} convert(f16[7424,128]{1,0:T(8,128)(2,1)S(1)} %all-gather.2) | non-fusion elementwise | flops 950272 | bytes 3801088 | tf_op jit(solution)/shard_map/convert_element_type | solution.py:276
  67.9 4.5 %shard_map.106 = (bf16[8,240,128]{2,1,0:T(8,128)(2,1)S(1)}, bf16[8,240,128]{2,1,0:T(8,128)(2,1)S(1)}, bf16[128,384]{1,0:T(8,128)(2,1)S(1)}) custom-call(s32[1]{0:T(128)} %bitcast.after_ref.core_ref, f32[8,128]{1,0:T(8,128)} %copy-done.8, bf16[16,464,128]{2,1,0:T(8,128)(2,1)} %bitcast.19, bf16[256,3584]{1,0:T(8,128)(2,1)} %get-tuple-element.28.wide_hbm, ...), custom_call_target="tpu_custom_call" | custom-call | bytes 7573508 | tf_op jit(solution)/shard_map/pallas_call | solution.py:222
  72.4 2.3 %collective-permute-start = (bf16[8,240,128]{2,1,0:T(8,128)(2,1)S(1)}, bf16[8,240,128]{2,1,0:T(8,128)(2,1)S(1)}, u32[]{:S(2)}, u32[]{:S(2)}) collective-permute-start(bf16[8,240,128]{2,1,0:T(8,128)(2,1)S(1)} %get-tuple-element.32), channel_id=1, source_target_pairs={{0,1},{1,0},{2,3},{3,2},{4,5},{5,4},{6,7},{7,6},{8,9},{9,8},{10,11... | collective-permute-start | bytes 1474568 | tf_op jit(solution)/shard_map/ppermute | solution.py:299
  74.8 1.7 %collective-permute-done = bf16[8,240,128]{2,1,0:T(8,128)(2,1)S(1)} collective-permute-done((bf16[8,240,128]{2,1,0:T(8,128)(2,1)S(1)}, bf16[8,240,128]{2,1,0:T(8,128)(2,1)S(1)}, u32[]{:S(2)}, u32[]{:S(2)}) %collective-permute-start) | collective-permute-done | bytes 491552 | tf_op jit(solution)/shard_map/ppermute | solution.py:299
  76.5 0.1 add_convert_fusion
  76.6 21.5 %all_to_all.15.parts_ref = bf16[8,240,128]{2,1,0:T(8,128)(2,1)S(1)} all-to-all(bf16[8,240,128]{2,1,0:T(8,128)(2,1)S(1)} %add_convert_fusion), channel_id=1, replica_groups={{0,2,4,6,8,10,12,14},{1,3,5,7,9,11,13,15},{16,18,20,22,24,26,28,30},{17..., dimensions={0} | all-to-all | bytes 983040 | tf_op jit(solution)/shard_map/all_to_all | solution.py:301
  98.1 0.8 shard_map.107
  99.0 5.7 %all-to-all-start.2 = ((bf16[64,4,128]{2,1,0:T(4,128)(2,1)}), bf16[64,4,128]{2,1,0:T(4,128)(2,1)S(1)}, u32[]{:S(2)}, u32[]{:S(2)}) async-start(bf16[64,4,128]{2,1,0:T(4,128)(2,1)} %bitcast.11), calls=%async_computation.2 | async-start | bytes 131072 | tf_op jit(solution)/shard_map/all_to_all | solution.py:309
  104.7 1.2 copy-done.4
  105.9 1.2 copy-done.5
  107.0 1.2 %shard_map.109 = f32[3,28,128]{2,1,0:T(8,128)S(1)} custom-call(bf16[16,464,128]{2,1,0:T(8,128)(2,1)S(1)} %bitcast.20, bf16[128,384]{1,0:T(8,128)(2,1)S(1)} %get-tuple-element.35.d_ref, bf16[3584,128]{1,0:T(8,128)(2,1)S(1)} %bitcast.22, bf16[3584,128]{1,0:T(8,128)(2,1)S(1)} %bitcast.24, bf16[3584,128]{1,0:T(8,128)(2,1)S(1)} %copy-done.5), custom_call_target="tpu_custom_call" | custom-call | bytes 4794368 | tf_op jit(solution)/shard_map/pallas_call | solution.py:222
  108.3 0.7 copy.11
  108.9 9.2 %all-to-all-done.2 = bf16[64,4,128]{2,1,0:T(4,128)(2,1)S(1)} async-done(((bf16[64,4,128]{2,1,0:T(4,128)(2,1)}), bf16[64,4,128]{2,1,0:T(4,128)(2,1)S(1)}, u32[]{:S(2)}, u32[]{:S(2)}) %all-to-all-start.2) | async-done | bytes 65568 | tf_op jit(solution)/shard_map/all_to_all | solution.py:309
  118.2 1.1 shard_map.108
  (14 shorter events, 0.1 us)
Async XLA Ops:
  2.8 36.8 %all-to-all-start = ((bf16[64,8,128]{2,1,0:T(8,128)(2,1)}), bf16[64,8,128]{2,1,0:T(8,128)(2,1)S(1)}, u32[]{:S(2)}, u32[]{:S(2)}) async-start(bf16[64,8,128]{2,1,0:T(8,128)(2,1)} %bitcast.32), calls=%async_computation | async-start | bytes 262144 | tf_op jit(solution)/shard_map/all_to_all | solution.py:256
  26.4 1.2 copy-start.1
  27.6 1.2 copy-start.3
  28.8 1.2 copy-start.6
  40.0 27.9 %copy-start.8 = (f32[8,128]{1,0:T(8,128)}, f32[8,128]{1,0:T(8,128)S(1)}, u32[]{:S(2)}) copy-start(f32[8,128]{1,0:T(8,128)S(1)} %get-tuple-element.26.prob_ref) | copy-start | bytes 12292
  72.4 32.2 %copy-start = (bf16[7424,128]{1,0:T(8,128)(2,1)S(1)}, bf16[7424,128]{1,0:T(8,128)(2,1)}, u32[]{:S(2)}) copy-start(bf16[7424,128]{1,0:T(8,128)(2,1)} %convert_element_type.20) | copy-start | bytes 5701636
  72.4 32.2 %copy-start.2 = (bf16[1,3584,128]{2,1,0:T(8,128)(2,1)S(1)}, bf16[1,3584,128]{2,1,0:T(8,128)(2,1)}, u32[]{:S(2)}) copy-start(bf16[1,3584,128]{2,1,0:T(8,128)(2,1)} %param.12) | copy-start | bytes 2752516
  72.4 4.0 %collective-permute-start = (bf16[8,240,128]{2,1,0:T(8,128)(2,1)S(1)}, bf16[8,240,128]{2,1,0:T(8,128)(2,1)S(1)}, u32[]{:S(2)}, u32[]{:S(2)}) collective-permute-start(bf16[8,240,128]{2,1,0:T(8,128)(2,1)S(1)} %get-tuple-element.32), channel_id=1, source_target_pairs={{0,1},{1,0},{2,3},{3,2},{4,5},{5,4},{6,7},{7,6},{8,9},{9,8},{10,11... | collective-permute-start | bytes 1474568 | tf_op jit(solution)/shard_map/ppermute | solution.py:299
  99.0 19.2 %all-to-all-start.2 = ((bf16[64,4,128]{2,1,0:T(4,128)(2,1)}), bf16[64,4,128]{2,1,0:T(4,128)(2,1)S(1)}, u32[]{:S(2)}, u32[]{:S(2)}) async-start(bf16[64,4,128]{2,1,0:T(4,128)(2,1)} %bitcast.11), calls=%async_computation.2 | async-start | bytes 131072 | tf_op jit(solution)/shard_map/all_to_all | solution.py:309
  104.7 1.2 copy-start.4
  105.9 1.2 copy-start.5
  107.0 11.1 %copy-start.7 = (s32[128,8]{0,1:T(8,128)S(1)}, s32[128,8]{0,1:T(8,128)}, u32[]{:S(2)}) copy-start(s32[128,8]{0,1:T(8,128)} %param.10) | copy-start | bytes 12292
where the time goes:
time: 120 us; the launch traced here: 119 us
  blocking collectives  47.9 us (40%)
  starting transfers between devices  30.8 us (26%)
  waiting for transfers between devices  17.2 us (14%)
  Pallas kernels  13.6 us (11%)
  local copies, waits for them, and re-layouts  7.36 us (6%)
  other arithmetic  1.64 us (1%)
    all_gather x1, blocking collectives, shards(): rows = lax.all_gather(xdy.astype(F16), 'local', axis=0).astype(BF16)  26.4 us
    all_to_all x1, starting transfers between devices, shards(): lax.all_to_all(sent.reshape(nodes, 8, LANES), 'node', 0, 0, tiled=True)  22.8 us
    all_to_all x1, blocking collectives, shards(): lax.all_to_all(pair, 'local', 0, 0, axis_index_groups=same_core, tiled=True)  21.5 us
    pallas_call x7, Pallas kernels, call(): pl.pallas_call(kernel, out_shape=outs, in_specs=specs, out_specs=[pl.Bloc...  13.6 us
    all_to_all x1, waiting for transfers between devices, shards(): lax.all_to_all(home.reshape(nodes, 4, LANES), 'node', 0, 0, tiled=True)  9.25 us
    unnamed x20, local copies, waits for them, and re-layouts  7.36 us
    all_to_all x1, waiting for transfers between devices, shards(): lax.all_to_all(sent.reshape(nodes, 8, LANES), 'node', 0, 0, tiled=True)  6.29 us
    all_to_all x1, starting transfers between devices, shards(): lax.all_to_all(home.reshape(nodes, 4, LANES), 'node', 0, 0, tiled=True)  5.68 us
  transfers between devices with their start and end apart: 3, of which 3 were waited for; matrix products, arithmetic and copies ran while one was open for 1% of the time, Pallas kernels for 4%

commit v1 on v0

--- a/solution.py
+++ b/solution.py
@@ -11,6 +11,7 @@
 LANES = 128
 TAIL = 16
 FACTORS = 3
+held = pltpu.with_memory_space_constraint
 F32 = jnp.float32
 F16 = jnp.float16
 BF16 = jnp.bfloat16
@@ -39,14 +40,32 @@
     return chosen, lax.rem(row, copies), matches
 
 
-def pack_kernel(routes_ref, probs_ref, x_ref, dy_ref, out_ref):
+def pack_kernel(
+    routes_hbm, probs_hbm, x_hbm, dy_hbm, out_ref, routes_ref, probs_ref, x_ref, dy_ref, sems
+):
+    pairs = (
+        (routes_hbm, routes_ref),
+        (probs_hbm, probs_ref),
+        (x_hbm, x_ref),
+        (dy_hbm, dy_ref),
+    )
+    moves = [
+        pltpu.make_async_copy(source, target, sems.at[i])
+        for i, (source, target) in enumerate(pairs)
+    ]
+    for move in moves:
+        move.start()
     rows, lanes = out_ref.shape
+    for move in moves[:2]:
+        move.wait()
     feats = x_ref.shape[0]
     chosen, block, matches = select_rows(routes_ref, 8, 4, rows)
     weight = jnp.zeros(chosen.shape, F32)
     for j, match in enumerate(matches):
         weight = jnp.where(match, probs_ref[j : j + 1, :].astype(F32), weight)
     weight = jnp.sum(weight * chosen, axis=1, keepdims=True)
+    for move in moves[2:]:
+        move.wait()
     pad = jnp.zeros((4 * lanes - 2 * feats, lanes), BF16)
     both = jnp.concatenate([x_ref[...], dy_ref[...], pad], axis=0)
     picked = dot(chosen.astype(BF16), both, LANES_BY_LANES)
@@ -120,23 +139,22 @@
 
 
 def main_kernel(
-    core_ref, prob_ref, rows_hbm, wide_hbm, down_hbm, tall_hbm,
-    keep_ref, send_ref, d_ref, rows_ref, wide_ref, down_ref, tall_ref, x_ref, dy_ref, sems,
+    core_ref, prob_ref, rows_ref, wide_hbm, down_hbm, tall_hbm,
+    keep_ref, send_ref, d_ref, wide_ref, down_ref, tall_ref, x_ref, dy_ref, sems,
 ):
-    pairs = ((rows_hbm, rows_ref), (wide_hbm, wide_ref), (down_hbm, down_ref), (tall_hbm, tall_ref))
+    pairs = ((wide_hbm, wide_ref), (down_hbm, down_ref), (tall_hbm, tall_ref))
     moves = [
         pltpu.make_async_copy(source, target, sems.at[i])
         for i, (source, target) in enumerate(pairs)
     ]
     for move in moves:
         move.start()
-    moves[0].wait()
     lower(rows_ref, x_ref, dy_ref)
     core = core_ref[0]
     hid = down_ref.shape[0]
+    moves[0].wait()
+    pre = dot(wide_ref[...], x_ref[...])
     moves[1].wait()
-    pre = dot(wide_ref[...], x_ref[...])
-    moves[2].wait()
     back = dot(down_ref[...], dy_ref[...])
     pre_gate, pre_up = pre[:hid], pre[hid:]
     prob = prob_ref[0:1, :]
@@ -155,7 +173,7 @@
     feats = x_ref.shape[0] // (2 * chips)
     line = lax.broadcasted_iota(jnp.int32, (rows - feats, lanes), 0)
     tail = jnp.where(line == 0, prob_term, 0.0).astype(BF16)
-    moves[3].wait()
+    moves[2].wait()
     for chip in range(chips):
         for target, rank in ((send_ref, 1 - core), (keep_ref, core)):
             start = pl.multiple_of((2 * chip + rank) * feats, 32)
@@ -197,21 +215,27 @@
     out_ref[...] = jnp.where(odd == 0, spread[:, :lanes], spread[:, lanes:]).astype(BF16)
 
 
-def finish_kernel(back_ref, routes_ref, tokens_ref, probs_ref):
-    rows, lanes = back_ref.shape
-    feats = tokens_ref.shape[0]
+def choose_kernel(routes_ref, out_ref):
+    rows = out_ref.shape[0]
+    tokens = routes_ref.shape[1]
     chosen, block, matches = select_rows(routes_ref, 4, 2, rows)
-    back = back_ref[...]
-    low = dot(back, jnp.where(block == 0, chosen, 0.0).astype(BF16), ROWS_BY_ROWS)
-    high_rows = jnp.where(block == 1, chosen, 0.0)
-    high = dot(back, high_rows.astype(BF16), ROWS_BY_ROWS)
-    tokens_ref[:lanes, :] = low.astype(BF16)
-    tokens_ref[lanes:, :] = high[: feats - lanes].astype(BF16)
-    given = back[:, feats - lanes : feats - lanes + 1].astype(F32) * high_rows
-    lines = [
-        jnp.sum(jnp.where(match, given, 0.0), axis=0, keepdims=True) for match in matches
-    ]
-    probs_ref[...] = jnp.concatenate(lines, axis=0).astype(BF16)
+    high = jnp.where(block == 1, chosen, 0.0)
+    masks = [jnp.where(block == 0, chosen, 0.0), high]
+    masks += [jnp.where(match, high, 0.0) for match in matches]
+    for i, mask in enumerate(masks):
+        out_ref[:, i * tokens : (i + 1) * tokens] = mask.astype(BF16)
+
+
+def finish_kernel(back_ref, chosen_ref, tokens_ref, probs_ref):
+    lanes = back_ref.shape[1]
+    feats, tokens = tokens_ref.shape
+    out = dot(back_ref[...], chosen_ref[...], ROWS_BY_ROWS)
+    tokens_ref[:lanes, :] = out[:, :tokens].astype(BF16)
+    tokens_ref[lanes:, :] = out[: feats - lanes, tokens : 2 * tokens].astype(BF16)
+    line = feats - lanes
+    for j in range(probs_ref.shape[0]):
+        part = slice((2 + j) * tokens, (3 + j) * tokens)
+        probs_ref[j : j + 1, :] = out[line : line + 1, part].astype(BF16)
 
 
 def call(kernel, outs, *args, scalars=0, scratch=(), limit=32, far=0):
@@ -247,11 +271,13 @@
     swap = [(i, i ^ 1) for i in range(local)]
     core = lax.rem(lax.axis_index("local"), 2).astype(jnp.int32).reshape(1)
 
+    given = (routes_t, gate_probs.T, tokens.T, cotangent.T)
     (sent,) = call(
         pack_kernel,
-        [shape((8 * nodes, LANES))],
-        routes_t, gate_probs.T, tokens.T, cotangent.T,
-        limit=60,
+        [pltpu.VMEM((8 * nodes, LANES), BF16)],
+        *[held(a, pltpu.HBM) for a in given],
+        scratch=[pltpu.VMEM(a.shape, a.dtype) for a in given] + [pltpu.SemaphoreType.DMA((4,))],
+        far=4,
     )
     got = lax.all_to_all(sent.reshape(nodes, 8, LANES), "node", 0, 0, tiled=True)
     later, _ = lax.optimization_barrier((core, sent))
@@ -282,19 +308,17 @@
             pltpu.VMEM((chips, high, slots), BF16),
             pltpu.VMEM((slots, 3 * hid), BF16),
         ],
-        core, prob, rows, wide, eff_down, tall,
+        core, prob, held(rows, pltpu.VMEM), *[held(a, pltpu.HBM) for a in (wide, eff_down, tall)],
         scalars=1,
         scratch=[
-            pltpu.VMEM(rows.shape, BF16),
             pltpu.VMEM((2 * hid, width), BF16),
             pltpu.VMEM((hid, width), BF16),
             pltpu.VMEM((width, 2 * hid), BF16),
             pltpu.VMEM((width, slots), BF16),
             pltpu.VMEM((width, slots), BF16),
-            pltpu.SemaphoreType.DMA((4,)),
+            pltpu.SemaphoreType.DMA((3,)),
         ],
-        far=4,
-        limit=57,
+        far=3,
     )
     came = lax.ppermute(send, "local", swap)
     pair = (keep.astype(F32) + came.astype(F32)).astype(BF16)
@@ -306,12 +330,15 @@
         scratch=[pltpu.VMEM((width, slots), BF16), pltpu.VMEM((width, slots), BF16)],
     )
     (home,) = call(collect_kernel, [shape((4 * nodes, LANES))], parts)
+    routes_later, home = lax.optimization_barrier((routes_t, home))
     back = lax.all_to_all(home.reshape(nodes, 4, LANES), "node", 0, 0, tiled=True)
+    top = routes.shape[1]
+    (chosen,) = call(choose_kernel, [shape((4 * nodes, (2 + top) * count))], routes_later)
     token_t, probs_t = call(
         finish_kernel,
-        [shape((feats, count)), shape((routes.shape[1], count))],
+        [shape((feats, count)), shape((top, count))],
         back.reshape(4 * nodes, LANES),
-        routes_t,
+        chosen,
     )
     return token_t.T, probs_t.T, noise_grad[None]
 

time: 120 us -> 117 us (0.975)
  other arithmetic: 1.64 us -> 0.37 us
    convert_element_type x2, other arithmetic: 1.51 us -> 0.23 us  [shards(): rows = lax.all_gather(xdy.astype(F16), 'local', axis=0).astype(BF16)]
    pallas_call x7 -> x8, Pallas kernels: 13.6 us -> 12.5 us  [call(): pl.pallas_call(kernel, out_shape=outs, in_specs=specs, out_specs=[pl.Bloc...]
    unnamed x20 -> x16, local copies, waits for them, and re-layouts: 7.36 us -> 7.35 us
where the time goes in v1:
time: 117 us
  blocking collectives  47.9 us (41%)
  starting transfers between devices  30.7 us (26%)
  waiting for transfers between devices  16.9 us (14%)
  Pallas kernels  12.5 us (11%)
  local copies, waits for them, and re-layouts  7.35 us (6%)
    all_gather x1, blocking collectives, shards(): rows = lax.all_gather(xdy.astype(F16), 'local', axis=0).astype(BF16)  26.4 us
    all_to_all x1, starting transfers between devices, shards(): lax.all_to_all(sent.reshape(nodes, 8, LANES), 'node', 0, 0, tiled=True)  22.8 us
    all_to_all x1, blocking collectives, shards(): lax.all_to_all(pair, 'local', 0, 0, axis_index_groups=same_core, tiled=True)  21.6 us
    pallas_call x8, Pallas kernels, call(): pl.pallas_call(kernel, out_shape=outs, in_specs=specs, out_specs=[pl.Bloc...  12.5 us
    all_to_all x1, waiting for transfers between devices, shards(): lax.all_to_all(home.reshape(nodes, 4, LANES), 'node', 0, 0, tiled=True)  8.92 us
    unnamed x16, local copies, waits for them, and re-layouts  7.35 us
    all_to_all x1, waiting for transfers between devices, shards(): lax.all_to_all(sent.reshape(nodes, 8, LANES), 'node', 0, 0, tiled=True)  6.26 us
    all_to_all x1, starting transfers between devices, shards(): lax.all_to_all(home.reshape(nodes, 4, LANES), 'node', 0, 0, tiled=True)  5.71 us
  transfers between devices with their start and end apart: 3, of which 3 were waited for; matrix products, arithmetic and copies ran while one was open for 1% of the time, Pallas kernels for 4%

profile of v1, /device:TPU:1, one launch (start us, length us, event | category | flops | bytes accessed | tf_op | source)
XLA Modules:
  0.0 116.5 jit_solution(18002073907297772993)
XLA Ops:
  0.6 2.3 %shard_map.103 = bf16[512,128]{1,0:T(8,128)(2,1)} custom-call(s32[8,128]{1,0:T(8,128)} %bitcast.30, bf16[8,128]{1,0:T(8,128)(2,1)} %bitcast.34, bf16[224,128]{1,0:T(8,128)(2,1)} %bitcast.32, bf16[224,128]{1,0:T(8,128)(2,1)} %bitcast.33), custom_call_target="tpu_custom_call" | custom-call | bytes 251904 | tf_op jit(solution)/shard_map/pallas_call | solution.py:246
  2.9 22.8 %all-to-all-start = ((bf16[64,8,128]{2,1,0:T(8,128)(2,1)}), bf16[64,8,128]{2,1,0:T(8,128)(2,1)S(1)}, u32[]{:S(2)}, u32[]{:S(2)}) async-start(bf16[64,8,128]{2,1,0:T(8,128)(2,1)} %bitcast.5), calls=%async_computation | async-start | bytes 262144 | tf_op jit(solution)/shard_map/all_to_all | solution.py:282
  25.7 0.8 copy.14
  26.5 1.2 %copy-done = bf16[1,3584,128]{2,1,0:T(8,128)(2,1)S(1)} copy-done((bf16[1,3584,128]{2,1,0:T(8,128)(2,1)S(1)}, bf16[1,3584,128]{2,1,0:T(8,128)(2,1)}, u32[]{:S(2)}) %copy-start) | copy-done | bytes 917528
  27.7 1.2 %copy-done.2 = bf16[1,3584,128]{2,1,0:T(8,128)(2,1)S(1)} copy-done((bf16[1,3584,128]{2,1,0:T(8,128)(2,1)S(1)}, bf16[1,3584,128]{2,1,0:T(8,128)(2,1)}, u32[]{:S(2)}) %copy-start.2) | copy-done | bytes 917528
  28.9 1.2 %copy-done.5 = bf16[1,128,3584]{2,1,0:T(8,128)(2,1)S(1)} copy-done((bf16[1,128,3584]{2,1,0:T(8,128)(2,1)S(1)}, bf16[1,128,3584]{2,1,0:T(8,128)(2,1)}, u32[]{:S(2)}) %copy-start.5) | copy-done | bytes 917528
  30.1 3.4 %shard_map.104 = (bf16[256,3584]{1,0:T(8,128)(2,1)}, bf16[3584,256]{1,0:T(8,128)(2,1)}, bf16[128,3584]{1,0:T(8,128)(2,1)}, bf16[3584,128]{1,0:T(8,128)(2,1)}) custom-call(s32[1]{0:T(128)} %bitcast.1.after_ref.core_ref, bf16[3584,128]{1,0:T(8,128)(2,1)S(1)} %bitcast.21, bf16[3584,128]{1,0:T(8,128)(2,1)S(1)} %bitcast.23, bf16[128,3584]{1,0:T(8,128)(2,1)S(1)} %bitcast.25, ...), custom_call_target="tpu_custom_call" | custom-call | bytes 8300548 | tf_op jit(solution)/shard_map/pallas_call | solution.py:246
  33.4 6.3 %all-to-all-done = bf16[64,8,128]{2,1,0:T(8,128)(2,1)S(1)} async-done(((bf16[64,8,128]{2,1,0:T(8,128)(2,1)}), bf16[64,8,128]{2,1,0:T(8,128)(2,1)S(1)}, u32[]{:S(2)}, u32[]{:S(2)}) %all-to-all-start) | async-done | bytes 131104 | tf_op jit(solution)/shard_map/all_to_all | solution.py:282
  39.7 0.4 shard_map.105
  40.1 26.4 %all-gather.2 = f16[7424,128]{1,0:T(8,128)(2,1)S(1)} all-gather(f16[464,128]{1,0:T(8,128)(2,1)S(1)} %convert_element_type.15), channel_id=2, replica_groups=mesh['node'=64,'local'=16] {'local'}, dimensions={0}, use_global_device_ids=true | all-gather | bytes 2019328 | tf_op jit(solution)/shard_map/all_gather | solution.py:302
  66.5 0.2 convert_element_type.20
  66.7 3.3 %shard_map.106 = (bf16[8,240,128]{2,1,0:T(8,128)(2,1)S(1)}, bf16[8,240,128]{2,1,0:T(8,128)(2,1)S(1)}, bf16[128,384]{1,0:T(8,128)(2,1)S(1)}) custom-call(s32[1]{0:T(128)} %bitcast.1.after_ref.core_ref, f32[8,128]{1,0:T(8,128)S(1)} %get-tuple-element.28.prob_ref, bf16[16,464,128]{2,1,0:T(8,128)(2,1)S(1)} %bitcast.19, ...), custom_call_target="tpu_custom_call" | custom-call | bytes 7573508 | tf_op jit(solution)/shard_map/pallas_call | solution.py:246
  70.0 2.2 %collective-permute-start = (bf16[8,240,128]{2,1,0:T(8,128)(2,1)S(1)}, bf16[8,240,128]{2,1,0:T(8,128)(2,1)S(1)}, u32[]{:S(2)}, u32[]{:S(2)}) collective-permute-start(bf16[8,240,128]{2,1,0:T(8,128)(2,1)S(1)} %get-tuple-element.34), channel_id=1, source_target_pairs={{0,1},{1,0},{2,3},{3,2},{4,5},{5,4},{6,7},{7,6},{8,9},{9,8},{10,11... | collective-permute-start | bytes 1474568 | tf_op jit(solution)/shard_map/ppermute | solution.py:323
  72.2 1.7 %collective-permute-done = bf16[8,240,128]{2,1,0:T(8,128)(2,1)S(1)} collective-permute-done((bf16[8,240,128]{2,1,0:T(8,128)(2,1)S(1)}, bf16[8,240,128]{2,1,0:T(8,128)(2,1)S(1)}, u32[]{:S(2)}, u32[]{:S(2)}) %collective-permute-start) | collective-permute-done | bytes 491552 | tf_op jit(solution)/shard_map/ppermute | solution.py:323
  74.0 21.6 %all_to_all.15.parts_ref = bf16[8,240,128]{2,1,0:T(8,128)(2,1)S(1)} all-to-all(bf16[8,240,128]{2,1,0:T(8,128)(2,1)S(1)} %add_convert_fusion), channel_id=1, replica_groups={{0,2,4,6,8,10,12,14},{1,3,5,7,9,11,13,15},{16,18,20,22,24,26,28,30},{17..., dimensions={0} | all-to-all | bytes 983040 | tf_op jit(solution)/shard_map/all_to_all | solution.py:325
  95.6 0.8 shard_map.107
  96.4 5.7 %all-to-all-start.2 = ((bf16[64,4,128]{2,1,0:T(4,128)(2,1)}), bf16[64,4,128]{2,1,0:T(4,128)(2,1)S(1)}, u32[]{:S(2)}, u32[]{:S(2)}) async-start(bf16[64,4,128]{2,1,0:T(4,128)(2,1)} %bitcast.11), calls=%async_computation.2 | async-start | bytes 131072 | tf_op jit(solution)/shard_map/all_to_all | solution.py:334
  102.2 1.2 %copy-done.3 = bf16[1,3584,128]{2,1,0:T(8,128)(2,1)S(1)} copy-done((bf16[1,3584,128]{2,1,0:T(8,128)(2,1)S(1)}, bf16[1,3584,128]{2,1,0:T(8,128)(2,1)}, u32[]{:S(2)}) %copy-start.3) | copy-done | bytes 917528
  103.3 1.2 %copy-done.4 = bf16[3584,128]{1,0:T(8,128)(2,1)S(1)} copy-done((bf16[3584,128]{1,0:T(8,128)(2,1)S(1)}, bf16[3584,128]{1,0:T(8,128)(2,1)}, u32[]{:S(2)}) %copy-start.4) | copy-done | bytes 917528
  104.5 1.2 %shard_map.110 = f32[3,28,128]{2,1,0:T(8,128)S(1)} custom-call(bf16[16,464,128]{2,1,0:T(8,128)(2,1)S(1)} %bitcast.20, bf16[128,384]{1,0:T(8,128)(2,1)S(1)} %get-tuple-element.39.d_ref, bf16[3584,128]{1,0:T(8,128)(2,1)S(1)} %bitcast.22, bf16[3584,128]{1,0:T(8,128)(2,1)S(1)} %bitcast.24, bf16[3584,128]{1,0:T(8,128)(2,1)S(1)} %copy-done.4), custom_call_target="tpu_custom_call" | custom-call | bytes 4794368 | tf_op jit(solution)/shard_map/pallas_call | solution.py:246
  105.7 0.7 copy.11
  106.4 0.3 shard_map.108.chosen_ref
  106.7 8.9 %all-to-all-done.2 = bf16[64,4,128]{2,1,0:T(4,128)(2,1)S(1)} async-done(((bf16[64,4,128]{2,1,0:T(4,128)(2,1)}), bf16[64,4,128]{2,1,0:T(4,128)(2,1)S(1)}, u32[]{:S(2)}, u32[]{:S(2)}) %all-to-all-start.2) | async-done | bytes 65568 | tf_op jit(solution)/shard_map/all_to_all | solution.py:334
  115.7 0.9 shard_map.109
  (11 shorter events, 0.2 us)
Async XLA Ops:
  2.9 36.8 %all-to-all-start = ((bf16[64,8,128]{2,1,0:T(8,128)(2,1)}), bf16[64,8,128]{2,1,0:T(8,128)(2,1)S(1)}, u32[]{:S(2)}, u32[]{:S(2)}) async-start(bf16[64,8,128]{2,1,0:T(8,128)(2,1)} %bitcast.5), calls=%async_computation | async-start | bytes 262144 | tf_op jit(solution)/shard_map/all_to_all | solution.py:282
  26.5 1.2 %copy-start = (bf16[1,3584,128]{2,1,0:T(8,128)(2,1)S(1)}, bf16[1,3584,128]{2,1,0:T(8,128)(2,1)}, u32[]{:S(2)}) copy-start(bf16[1,3584,128]{2,1,0:T(8,128)(2,1)} %param.12) | copy-start | bytes 2752516
  27.7 1.2 %copy-start.2 = (bf16[1,3584,128]{2,1,0:T(8,128)(2,1)S(1)}, bf16[1,3584,128]{2,1,0:T(8,128)(2,1)}, u32[]{:S(2)}) copy-start(bf16[1,3584,128]{2,1,0:T(8,128)(2,1)} %param.13) | copy-start | bytes 2752516
  28.9 1.2 %copy-start.5 = (bf16[1,128,3584]{2,1,0:T(8,128)(2,1)S(1)}, bf16[1,128,3584]{2,1,0:T(8,128)(2,1)}, u32[]{:S(2)}) copy-start(bf16[1,128,3584]{2,1,0:T(8,128)(2,1)} %param.14) | copy-start | bytes 2752516
  70.0 32.2 %copy-start.1 = (bf16[1,3584,128]{2,1,0:T(8,128)(2,1)S(1)}, bf16[1,3584,128]{2,1,0:T(8,128)(2,1)}, u32[]{:S(2)}) copy-start(bf16[1,3584,128]{2,1,0:T(8,128)(2,1)} %param.12) | copy-start | bytes 2752516
  70.0 3.9 %collective-permute-start = (bf16[8,240,128]{2,1,0:T(8,128)(2,1)S(1)}, bf16[8,240,128]{2,1,0:T(8,128)(2,1)S(1)}, u32[]{:S(2)}, u32[]{:S(2)}) collective-permute-start(bf16[8,240,128]{2,1,0:T(8,128)(2,1)S(1)} %get-tuple-element.34), channel_id=1, source_target_pairs={{0,1},{1,0},{2,3},{3,2},{4,5},{5,4},{6,7},{7,6},{8,9},{9,8},{10,11... | collective-permute-start | bytes 1474568 | tf_op jit(solution)/shard_map/ppermute | solution.py:323
  96.4 19.2 %all-to-all-start.2 = ((bf16[64,4,128]{2,1,0:T(4,128)(2,1)}), bf16[64,4,128]{2,1,0:T(4,128)(2,1)S(1)}, u32[]{:S(2)}, u32[]{:S(2)}) async-start(bf16[64,4,128]{2,1,0:T(4,128)(2,1)} %bitcast.11), calls=%async_computation.2 | async-start | bytes 131072 | tf_op jit(solution)/shard_map/all_to_all | solution.py:334
  102.1 1.2 %copy-start.3 = (bf16[1,3584,128]{2,1,0:T(8,128)(2,1)S(1)}, bf16[1,3584,128]{2,1,0:T(8,128)(2,1)}, u32[]{:S(2)}) copy-start(bf16[1,3584,128]{2,1,0:T(8,128)(2,1)} %param.13) | copy-start | bytes 2752516
  103.3 1.2 %copy-start.4 = (bf16[3584,128]{1,0:T(8,128)(2,1)S(1)}, bf16[3584,128]{1,0:T(8,128)(2,1)}, u32[]{:S(2)}) copy-start(bf16[3584,128]{1,0:T(8,128)(2,1)} %get-tuple-element.40.down_t_ref) | copy-start | bytes 2752516
  104.5 1.9 %copy-start.6 = (s32[128,8]{0,1:T(8,128)S(1)}, s32[128,8]{0,1:T(8,128)}, u32[]{:S(2)}) copy-start(s32[128,8]{0,1:T(8,128)} %param.10) | copy-start | bytes 12292

commit v2 on v1

--- a/solution.py
+++ b/solution.py
@@ -108,7 +108,7 @@
 
 
 def scale_kernel(
-    after_ref, gate_ref, up_ref, down_ref, noise_ref, wide_ref, tall_ref, eff_down_ref, down_t_ref
+    after_ref, gate_ref, up_ref, down_ref, noise_ref, tall_ref, eff_down_ref, down_t_ref
 ):
     del after_ref
     blocks, lanes = noise_ref.shape[1:]
@@ -118,8 +118,6 @@
         up = up_ref[part, :].astype(F32) * (1.0 + noise_ref[1, b : b + 1, :])
         tall_ref[part, :lanes] = gate.astype(BF16)
         tall_ref[part, lanes:] = up.astype(BF16)
-        wide_ref[:lanes, part] = gate.astype(BF16).T
-        wide_ref[lanes:, part] = up.astype(BF16).T
         down = down_ref[:, part].T
         down_t_ref[part, :] = down
         back = down.astype(F32) * (1.0 + noise_ref[2, b : b + 1, :])
@@ -139,10 +137,10 @@
 
 
 def main_kernel(
-    core_ref, prob_ref, rows_ref, wide_hbm, down_hbm, tall_hbm,
-    keep_ref, send_ref, d_ref, wide_ref, down_ref, tall_ref, x_ref, dy_ref, sems,
+    core_ref, prob_ref, rows_ref, tall_hbm, down_hbm,
+    keep_ref, send_ref, d_ref, tall_ref, down_ref, x_ref, dy_ref, sems,
 ):
-    pairs = ((wide_hbm, wide_ref), (down_hbm, down_ref), (tall_hbm, tall_ref))
+    pairs = ((tall_hbm, tall_ref), (down_hbm, down_ref))
     moves = [
         pltpu.make_async_copy(source, target, sems.at[i])
         for i, (source, target) in enumerate(pairs)
@@ -153,7 +151,7 @@
     core = core_ref[0]
     hid = down_ref.shape[0]
     moves[0].wait()
-    pre = dot(wide_ref[...], x_ref[...])
+    pre = dot(x_ref[...], tall_ref[...], ROWS_BY_ROWS).T
     moves[1].wait()
     back = dot(down_ref[...], dy_ref[...])
     pre_gate, pre_up = pre[:hid], pre[hid:]
@@ -173,7 +171,6 @@
     feats = x_ref.shape[0] // (2 * chips)
     line = lax.broadcasted_iota(jnp.int32, (rows - feats, lanes), 0)
     tail = jnp.where(line == 0, prob_term, 0.0).astype(BF16)
-    moves[2].wait()
     for chip in range(chips):
         for target, rank in ((send_ref, 1 - core), (keep_ref, core)):
             start = pl.multiple_of((2 * chip + rank) * feats, 32)
@@ -284,7 +281,6 @@
     scaled = call(
         scale_kernel,
         [
-            pltpu.HBM((2 * hid, width), BF16),
             pltpu.HBM((width, 2 * hid), BF16),
             pltpu.HBM((hid, width), BF16),
             pltpu.HBM((width, hid), BF16),
@@ -293,7 +289,7 @@
         scalars=1,
     )
     got, scaled = lax.optimization_barrier((got, scaled))
-    wide, tall, eff_down, down_t = scaled
+    tall, eff_down, down_t = scaled
     xdy, prob = call(
         unpack_kernel,
         [shape((2 * feats + TAIL, slots), F32), shape((8, slots), F32)],
@@ -308,17 +304,16 @@
             pltpu.VMEM((chips, high, slots), BF16),
             pltpu.VMEM((slots, 3 * hid), BF16),
         ],
-        core, prob, held(rows, pltpu.VMEM), *[held(a, pltpu.HBM) for a in (wide, eff_down, tall)],
+        core, prob, held(rows, pltpu.VMEM), *[held(a, pltpu.HBM) for a in (tall, eff_down)],
         scalars=1,
         scratch=[
-            pltpu.VMEM((2 * hid, width), BF16),
+            pltpu.VMEM((width, 2 * hid), BF16),
             pltpu.VMEM((hid, width), BF16),
-            pltpu.VMEM((width, 2 * hid), BF16),
             pltpu.VMEM((width, slots), BF16),
             pltpu.VMEM((width, slots), BF16),
-            pltpu.SemaphoreType.DMA((3,)),
+            pltpu.SemaphoreType.DMA((2,)),
         ],
-        far=3,
+        far=2,
     )
     came = lax.ppermute(send, "local", swap)
     pair = (keep.astype(F32) + came.astype(F32)).astype(BF16)

time: 117 us -> 117 us (level)
  transfers between devices with their start and end apart: 3 -> 3, of which waited for: 3 -> 3; matrix products, arithmetic and copies ran while one was open for 1% -> 1% of each run, Pallas kernels for 4% -> 3%
where the time goes in v2:
time: 117 us; the launch traced here: 116 us
  blocking collectives  47.9 us (41%)
  starting transfers between devices  30.2 us (26%)
  waiting for transfers between devices  17.8 us (15%)
  Pallas kernels  11.8 us (10%)
  local copies, waits for them, and re-layouts  7.35 us (6%)
    all_gather x1, blocking collectives, shards(): rows = lax.all_gather(xdy.astype(F16), 'local', axis=0).astype(BF16)  26.4 us
    all_to_all x1, starting transfers between devices, shards(): lax.all_to_all(sent.reshape(nodes, 8, LANES), 'node', 0, 0, tiled=True)  22.8 us
    all_to_all x1, blocking collectives, shards(): lax.all_to_all(pair, 'local', 0, 0, axis_index_groups=same_core, tiled=True)  21.5 us
    pallas_call x8, Pallas kernels, call(): pl.pallas_call(kernel, out_shape=outs, in_specs=specs, out_specs=[pl.Bloc...  11.8 us
    all_to_all x1, waiting for transfers between devices, shards(): lax.all_to_all(home.reshape(nodes, 4, LANES), 'node', 0, 0, tiled=True)  8.92 us
    unnamed x16, local copies, waits for them, and re-layouts  7.35 us
    all_to_all x1, waiting for transfers between devices, shards(): lax.all_to_all(sent.reshape(nodes, 8, LANES), 'node', 0, 0, tiled=True)  7.2 us
    all_to_all x1, starting transfers between devices, shards(): lax.all_to_all(home.reshape(nodes, 4, LANES), 'node', 0, 0, tiled=True)  5.26 us
  transfers between devices with their start and end apart: 3, of which 3 were waited for; matrix products, arithmetic and copies ran while one was open for 1% of the time, Pallas kernels for 3%

profile of v2, /device:TPU:1, one launch (start us, length us, event | category | flops | bytes accessed | tf_op | source)
XLA Modules:
  0.0 116.2 jit_solution(17193709983647236152)
XLA Ops:
  0.6 2.3 %shard_map.103 = bf16[512,128]{1,0:T(8,128)(2,1)} custom-call(s32[8,128]{1,0:T(8,128)} %bitcast.30, bf16[8,128]{1,0:T(8,128)(2,1)} %bitcast.34, bf16[224,128]{1,0:T(8,128)(2,1)} %bitcast.32, bf16[224,128]{1,0:T(8,128)(2,1)} %bitcast.33), custom_call_target="tpu_custom_call" | custom-call | bytes 251904 | tf_op jit(solution)/shard_map/pallas_call | solution.py:243
  2.9 22.8 %all-to-all-start = ((bf16[64,8,128]{2,1,0:T(8,128)(2,1)}), bf16[64,8,128]{2,1,0:T(8,128)(2,1)S(1)}, u32[]{:S(2)}, u32[]{:S(2)}) async-start(bf16[64,8,128]{2,1,0:T(8,128)(2,1)} %bitcast.5), calls=%async_computation | async-start | bytes 262144 | tf_op jit(solution)/shard_map/all_to_all | solution.py:279
  25.7 0.8 copy.14
  26.5 1.2 %copy-done = bf16[1,3584,128]{2,1,0:T(8,128)(2,1)S(1)} copy-done((bf16[1,3584,128]{2,1,0:T(8,128)(2,1)S(1)}, bf16[1,3584,128]{2,1,0:T(8,128)(2,1)}, u32[]{:S(2)}) %copy-start) | copy-done | bytes 917528
  27.7 1.2 %copy-done.2 = bf16[1,3584,128]{2,1,0:T(8,128)(2,1)S(1)} copy-done((bf16[1,3584,128]{2,1,0:T(8,128)(2,1)S(1)}, bf16[1,3584,128]{2,1,0:T(8,128)(2,1)}, u32[]{:S(2)}) %copy-start.2) | copy-done | bytes 917528
  28.9 1.2 %copy-done.5 = bf16[1,128,3584]{2,1,0:T(8,128)(2,1)S(1)} copy-done((bf16[1,128,3584]{2,1,0:T(8,128)(2,1)S(1)}, bf16[1,128,3584]{2,1,0:T(8,128)(2,1)}, u32[]{:S(2)}) %copy-start.5) | copy-done | bytes 917528
  30.0 2.4 %shard_map.104 = (bf16[3584,256]{1,0:T(8,128)(2,1)}, bf16[128,3584]{1,0:T(8,128)(2,1)}, bf16[3584,128]{1,0:T(8,128)(2,1)}) custom-call(s32[1]{0:T(128)} %bitcast.1.after_ref.core_ref, bf16[3584,128]{1,0:T(8,128)(2,1)S(1)} %bitcast.21, bf16[3584,128]{1,0:T(8,128)(2,1)S(1)} %bitcast.23, bf16[128,3584]{1,0:T(8,128)(2,1)S(1)} %bitcast.25, f32[3,28,128]{2,1,0:T(8,128)S(1)} %bitcast.29), custom_call_target="tpu_custom_call" | custom-call | bytes 6465540 | tf_op jit(solution)/shard_map/pallas_call | solution.py:243
  32.5 7.2 %all-to-all-done = bf16[64,8,128]{2,1,0:T(8,128)(2,1)S(1)} async-done(((bf16[64,8,128]{2,1,0:T(8,128)(2,1)}), bf16[64,8,128]{2,1,0:T(8,128)(2,1)S(1)}, u32[]{:S(2)}, u32[]{:S(2)}) %all-to-all-start) | async-done | bytes 131104 | tf_op jit(solution)/shard_map/all_to_all | solution.py:279
  39.7 0.4 shard_map.105
  40.1 26.4 %all-gather.2 = f16[7424,128]{1,0:T(8,128)(2,1)S(1)} all-gather(f16[464,128]{1,0:T(8,128)(2,1)S(1)} %convert_element_type.15), channel_id=2, replica_groups=mesh['node'=64,'local'=16] {'local'}, dimensions={0}, use_global_device_ids=true | all-gather | bytes 2019328 | tf_op jit(solution)/shard_map/all_gather | solution.py:298
  66.5 0.2 convert_element_type.20
  66.7 3.5 %shard_map.106 = (bf16[8,240,128]{2,1,0:T(8,128)(2,1)S(1)}, bf16[8,240,128]{2,1,0:T(8,128)(2,1)S(1)}, bf16[128,384]{1,0:T(8,128)(2,1)S(1)}) custom-call(s32[1]{0:T(128)} %bitcast.1.after_ref.core_ref, f32[8,128]{1,0:T(8,128)S(1)} %get-tuple-element.25.prob_ref, bf16[16,464,128]{2,1,0:T(8,128)(2,1)S(1)} %bitcast.19, ...), custom_call_target="tpu_custom_call" | custom-call | bytes 5738500 | tf_op jit(solution)/shard_map/pallas_call | solution.py:243
  70.2 2.2 %collective-permute-start = (bf16[8,240,128]{2,1,0:T(8,128)(2,1)S(1)}, bf16[8,240,128]{2,1,0:T(8,128)(2,1)S(1)}, u32[]{:S(2)}, u32[]{:S(2)}) collective-permute-start(bf16[8,240,128]{2,1,0:T(8,128)(2,1)S(1)} %get-tuple-element.30), channel_id=1, source_target_pairs={{0,1},{1,0},{2,3},{3,2},{4,5},{5,4},{6,7},{7,6},{8,9},{9,8},{10,11... | collective-permute-start | bytes 1474568 | tf_op jit(solution)/shard_map/ppermute | solution.py:318
  72.4 1.7 %collective-permute-done = bf16[8,240,128]{2,1,0:T(8,128)(2,1)S(1)} collective-permute-done((bf16[8,240,128]{2,1,0:T(8,128)(2,1)S(1)}, bf16[8,240,128]{2,1,0:T(8,128)(2,1)S(1)}, u32[]{:S(2)}, u32[]{:S(2)}) %collective-permute-start) | collective-permute-done | bytes 491552 | tf_op jit(solution)/shard_map/ppermute | solution.py:318
  74.2 21.5 %all_to_all.15.parts_ref = bf16[8,240,128]{2,1,0:T(8,128)(2,1)S(1)} all-to-all(bf16[8,240,128]{2,1,0:T(8,128)(2,1)S(1)} %add_convert_fusion), channel_id=1, replica_groups={{0,2,4,6,8,10,12,14},{1,3,5,7,9,11,13,15},{16,18,20,22,24,26,28,30},{17..., dimensions={0} | all-to-all | bytes 983040 | tf_op jit(solution)/shard_map/all_to_all | solution.py:320
  95.7 0.8 shard_map.107
  96.6 5.3 %all-to-all-start.2 = ((bf16[64,4,128]{2,1,0:T(4,128)(2,1)}), bf16[64,4,128]{2,1,0:T(4,128)(2,1)S(1)}, u32[]{:S(2)}, u32[]{:S(2)}) async-start(bf16[64,4,128]{2,1,0:T(4,128)(2,1)} %bitcast.11), calls=%async_computation.2 | async-start | bytes 131072 | tf_op jit(solution)/shard_map/all_to_all | solution.py:329
  101.9 1.2 %copy-done.3 = bf16[1,3584,128]{2,1,0:T(8,128)(2,1)S(1)} copy-done((bf16[1,3584,128]{2,1,0:T(8,128)(2,1)S(1)}, bf16[1,3584,128]{2,1,0:T(8,128)(2,1)}, u32[]{:S(2)}) %copy-start.3) | copy-done | bytes 917528
  103.0 1.2 %copy-done.4 = bf16[3584,128]{1,0:T(8,128)(2,1)S(1)} copy-done((bf16[3584,128]{1,0:T(8,128)(2,1)S(1)}, bf16[3584,128]{1,0:T(8,128)(2,1)}, u32[]{:S(2)}) %copy-start.4) | copy-done | bytes 917528
  104.2 1.2 %shard_map.110 = f32[3,28,128]{2,1,0:T(8,128)S(1)} custom-call(bf16[16,464,128]{2,1,0:T(8,128)(2,1)S(1)} %bitcast.20, bf16[128,384]{1,0:T(8,128)(2,1)S(1)} %get-tuple-element.35.d_ref, bf16[3584,128]{1,0:T(8,128)(2,1)S(1)} %bitcast.22, bf16[3584,128]{1,0:T(8,128)(2,1)S(1)} %bitcast.24, bf16[3584,128]{1,0:T(8,128)(2,1)S(1)} %copy-done.4), custom_call_target="tpu_custom_call" | custom-call | bytes 4794368 | tf_op jit(solution)/shard_map/pallas_call | solution.py:243
  105.4 0.7 copy.11
  106.1 0.3 shard_map.108.chosen_ref
  106.4 8.9 %all-to-all-done.2 = bf16[64,4,128]{2,1,0:T(4,128)(2,1)S(1)} async-done(((bf16[64,4,128]{2,1,0:T(4,128)(2,1)}), bf16[64,4,128]{2,1,0:T(4,128)(2,1)S(1)}, u32[]{:S(2)}, u32[]{:S(2)}) %all-to-all-start.2) | async-done | bytes 65568 | tf_op jit(solution)/shard_map/all_to_all | solution.py:329
  115.4 0.9 shard_map.109
  (11 shorter events, 0.2 us)
Async XLA Ops:
  2.9 36.8 %all-to-all-start = ((bf16[64,8,128]{2,1,0:T(8,128)(2,1)}), bf16[64,8,128]{2,1,0:T(8,128)(2,1)S(1)}, u32[]{:S(2)}, u32[]{:S(2)}) async-start(bf16[64,8,128]{2,1,0:T(8,128)(2,1)} %bitcast.5), calls=%async_computation | async-start | bytes 262144 | tf_op jit(solution)/shard_map/all_to_all | solution.py:279
  26.5 1.2 %copy-start = (bf16[1,3584,128]{2,1,0:T(8,128)(2,1)S(1)}, bf16[1,3584,128]{2,1,0:T(8,128)(2,1)}, u32[]{:S(2)}) copy-start(bf16[1,3584,128]{2,1,0:T(8,128)(2,1)} %param.12) | copy-start | bytes 2752516
  27.7 1.2 %copy-start.2 = (bf16[1,3584,128]{2,1,0:T(8,128)(2,1)S(1)}, bf16[1,3584,128]{2,1,0:T(8,128)(2,1)}, u32[]{:S(2)}) copy-start(bf16[1,3584,128]{2,1,0:T(8,128)(2,1)} %param.13) | copy-start | bytes 2752516
  28.9 1.2 %copy-start.5 = (bf16[1,128,3584]{2,1,0:T(8,128)(2,1)S(1)}, bf16[1,128,3584]{2,1,0:T(8,128)(2,1)}, u32[]{:S(2)}) copy-start(bf16[1,128,3584]{2,1,0:T(8,128)(2,1)} %param.14) | copy-start | bytes 2752516
  70.2 31.7 %copy-start.1 = (bf16[1,3584,128]{2,1,0:T(8,128)(2,1)S(1)}, bf16[1,3584,128]{2,1,0:T(8,128)(2,1)}, u32[]{:S(2)}) copy-start(bf16[1,3584,128]{2,1,0:T(8,128)(2,1)} %param.12) | copy-start | bytes 2752516
  70.2 3.9 %collective-permute-start = (bf16[8,240,128]{2,1,0:T(8,128)(2,1)S(1)}, bf16[8,240,128]{2,1,0:T(8,128)(2,1)S(1)}, u32[]{:S(2)}, u32[]{:S(2)}) collective-permute-start(bf16[8,240,128]{2,1,0:T(8,128)(2,1)S(1)} %get-tuple-element.30), channel_id=1, source_target_pairs={{0,1},{1,0},{2,3},{3,2},{4,5},{5,4},{6,7},{7,6},{8,9},{9,8},{10,11... | collective-permute-start | bytes 1474568 | tf_op jit(solution)/shard_map/ppermute | solution.py:318
  96.6 18.8 %all-to-all-start.2 = ((bf16[64,4,128]{2,1,0:T(4,128)(2,1)}), bf16[64,4,128]{2,1,0:T(4,128)(2,1)S(1)}, u32[]{:S(2)}, u32[]{:S(2)}) async-start(bf16[64,4,128]{2,1,0:T(4,128)(2,1)} %bitcast.11), calls=%async_computation.2 | async-start | bytes 131072 | tf_op jit(solution)/shard_map/all_to_all | solution.py:329
  101.9 1.2 %copy-start.3 = (bf16[1,3584,128]{2,1,0:T(8,128)(2,1)S(1)}, bf16[1,3584,128]{2,1,0:T(8,128)(2,1)}, u32[]{:S(2)}) copy-start(bf16[1,3584,128]{2,1,0:T(8,128)(2,1)} %param.13) | copy-start | bytes 2752516
  103.0 1.2 %copy-start.4 = (bf16[3584,128]{1,0:T(8,128)(2,1)S(1)}, bf16[3584,128]{1,0:T(8,128)(2,1)}, u32[]{:S(2)}) copy-start(bf16[3584,128]{1,0:T(8,128)(2,1)} %get-tuple-element.36.down_t_ref) | copy-start | bytes 2752516
  104.2 1.9 %copy-start.6 = (s32[128,8]{0,1:T(8,128)S(1)}, s32[128,8]{0,1:T(8,128)}, u32[]{:S(2)}) copy-start(s32[128,8]{0,1:T(8,128)} %param.10) | copy-start | bytes 12292

commit v3 on v2

--- a/solution.py
+++ b/solution.py
@@ -8,6 +8,9 @@
 from jax.sharding import PartitionSpec as P
 
 EXP_GROUP = 4
+DEPTH = 16
+NODE = ("x", "z")
+LOCAL = ("y", "core")
 LANES = 128
 TAIL = 16
 FACTORS = 3
@@ -23,21 +26,18 @@
     return lax.dot_general(a, b, dims, preferred_element_type=F32)
 
 
-def select_rows(routes_ref, per_group, copies, rows):
+def select_rows(routes_ref, group, slot):
     top, tokens = routes_ref.shape
-    row = lax.broadcasted_iota(jnp.int32, (rows, tokens), 0)
-    first = lax.div(row, per_group) * EXP_GROUP
-    slot = lax.rem(lax.div(row, copies), per_group // copies)
+    first = group * EXP_GROUP
     matches = [routes_ref[j : j + 1, :] == first for j in range(top)]
-    hit = jnp.zeros((rows, tokens), F32)
+    hit = jnp.zeros(group.shape, F32)
     for match in matches:
         hit = jnp.where(match, 1.0, hit)
     before = lax.broadcasted_iota(jnp.int32, (tokens, tokens), 0)
     after = lax.broadcasted_iota(jnp.int32, (tokens, tokens), 1)
     earlier = jnp.where(before < after, 1.0, 0.0).astype(BF16)
     rank = dot(hit.astype(BF16), earlier)
-    chosen = jnp.where(rank == slot.astype(F32), hit, 0.0)
-    return chosen, lax.rem(row, copies), matches
+    return jnp.where(rank == slot.astype(F32), hit, 0.0), matches
 
 
 def pack_kernel(
@@ -59,7 +59,9 @@
     for move in moves[:2]:
         move.wait()
     feats = x_ref.shape[0]
-    chosen, block, matches = select_rows(routes_ref, 8, 4, rows)
+    row = lax.broadcasted_iota(jnp.int32, (rows, lanes), 0)
+    block = lax.rem(row, 4)
+    chosen, matches = select_rows(routes_ref, lax.div(row, 8), lax.rem(lax.div(row, 4), 2))
     weight = jnp.zeros(chosen.shape, F32)
     for j, match in enumerate(matches):
         weight = jnp.where(match, probs_ref[j : j + 1, :].astype(F32), weight)
@@ -140,7 +142,8 @@
     core_ref, prob_ref, rows_ref, tall_hbm, down_hbm,
     keep_ref, send_ref, d_ref, tall_ref, down_ref, x_ref, dy_ref, sems,
 ):
-    pairs = ((tall_hbm, tall_ref), (down_hbm, down_ref))
+    width = tall_hbm.shape[0]
+    pairs = ((tall_hbm, tall_ref.at[pl.ds(0, width)]), (down_hbm, down_ref))
     moves = [
         pltpu.make_async_copy(source, target, sems.at[i])
         for i, (source, target) in enumerate(pairs)
@@ -151,7 +154,7 @@
     core = core_ref[0]
     hid = down_ref.shape[0]
     moves[0].wait()
-    pre = dot(x_ref[...], tall_ref[...], ROWS_BY_ROWS).T
+    pre = dot(x_ref[...], tall_ref[:width, :], ROWS_BY_ROWS).T
     moves[1].wait()
     back = dot(down_ref[...], dy_ref[...])
     pre_gate, pre_up = pre[:hid], pre[hid:]
@@ -165,17 +168,18 @@
     d_ref[:, :hid] = d_gate.T.astype(BF16)
     d_ref[:, hid : 2 * hid] = d_up.T.astype(BF16)
     d_ref[:, 2 * hid :] = (prob * hidden).T.astype(BF16)
-    d_both = jnp.concatenate([d_gate.astype(BF16), d_up.astype(BF16)], axis=0)
-    prob_term = jnp.sum(hidden * back, axis=0, keepdims=True)
-    chips, rows, lanes = keep_ref.shape
+    term = jnp.sum((hidden * back).T, axis=1, keepdims=True)
+    columns, chips, rows, lanes = keep_ref.shape
     feats = x_ref.shape[0] // (2 * chips)
-    line = lax.broadcasted_iota(jnp.int32, (rows - feats, lanes), 0)
-    tail = jnp.where(line == 0, prob_term, 0.0).astype(BF16)
+    lane = lax.broadcasted_iota(jnp.int32, (columns * rows, lanes), 1)
+    last = jnp.where(lane == feats, term, 0.0)
     for chip in range(chips):
         for target, rank in ((send_ref, 1 - core), (keep_ref, core)):
             start = pl.multiple_of((2 * chip + rank) * feats, 32)
-            target[chip, :feats, :] = dot(tall_ref[pl.ds(start, feats), :], d_both).astype(BF16)
-            target[chip, feats:, :] = tail
+            value = dot(d_ref[:, : 2 * hid], tall_ref[pl.ds(start, lanes), :], LANES_BY_LANES)
+            value = jnp.where(lane < feats, value, last).astype(BF16)
+            for column in range(columns):
+                target[column, chip] = value[column * rows : (column + 1) * rows]
 
 
 def noise_kernel(rows_ref, d_ref, gate_ref, up_ref, down_t_ref, out_ref, x_ref, dy_ref):
@@ -197,42 +201,43 @@
 
 
 def collect_kernel(parts_ref, out_ref):
-    rows, lanes = out_ref.shape
-    chips, height, slots = parts_ref.shape
-    total = parts_ref[0].astype(F32)
-    for chip in range(1, chips):
-        total = total + parts_ref[chip].astype(F32)
-    pad = jnp.zeros((2 * lanes - height, slots), BF16)
-    total = jnp.concatenate([total.astype(BF16), pad], axis=0)
-    row = lax.broadcasted_iota(jnp.int32, (rows, slots), 0)
-    col = lax.broadcasted_iota(jnp.int32, (rows, slots), 1)
-    place = jnp.where(lax.div(row, 2) == col, 1.0, 0.0).astype(BF16)
-    spread = dot(place, total, LANES_BY_LANES)
-    odd = lax.rem(lax.broadcasted_iota(jnp.int32, (rows, lanes), 0), 2)
-    out_ref[...] = jnp.where(odd == 0, spread[:, :lanes], spread[:, lanes:]).astype(BF16)
+    rows = out_ref.shape[0]
+    depth = parts_ref.shape[1]
+    columns = rows // depth
+    chips = parts_ref.shape[0] // columns
+    sums = []
+    for column in range(columns):
+        total = parts_ref[column * chips].astype(F32)
+        for chip in range(1, chips):
+            total = total + parts_ref[column * chips + chip].astype(F32)
+        sums.append(total.astype(BF16))
+    row = lax.broadcasted_iota(jnp.int32, (rows, rows), 0)
+    col = lax.broadcasted_iota(jnp.int32, (rows, rows), 1)
+    source = lax.rem(lax.div(row, 2), columns) * depth
+    source = source + 2 * lax.div(row, 2 * columns) + lax.rem(row, 2)
+    place = jnp.where(col == source, 1.0, 0.0).astype(BF16)
+    out_ref[...] = dot(place, jnp.concatenate(sums, axis=0)).astype(BF16)
 
 
 def choose_kernel(routes_ref, out_ref):
     rows = out_ref.shape[0]
     tokens = routes_ref.shape[1]
-    chosen, block, matches = select_rows(routes_ref, 4, 2, rows)
-    high = jnp.where(block == 1, chosen, 0.0)
-    masks = [jnp.where(block == 0, chosen, 0.0), high]
-    masks += [jnp.where(match, high, 0.0) for match in matches]
+    columns = rows // (2 * DEPTH)
+    row = lax.broadcasted_iota(jnp.int32, (rows, tokens), 0)
+    group = lax.rem(lax.div(row, 2), columns) * DEPTH + lax.div(row, 2 * columns)
+    chosen, matches = select_rows(routes_ref, group, lax.rem(row, 2))
+    masks = [chosen] + [jnp.where(match, chosen, 0.0) for match in matches]
     for i, mask in enumerate(masks):
         out_ref[:, i * tokens : (i + 1) * tokens] = mask.astype(BF16)
 
 
 def finish_kernel(back_ref, chosen_ref, tokens_ref, probs_ref):
-    lanes = back_ref.shape[1]
     feats, tokens = tokens_ref.shape
     out = dot(back_ref[...], chosen_ref[...], ROWS_BY_ROWS)
-    tokens_ref[:lanes, :] = out[:, :tokens].astype(BF16)
-    tokens_ref[lanes:, :] = out[: feats - lanes, tokens : 2 * tokens].astype(BF16)
-    line = feats - lanes
+    tokens_ref[...] = out[:feats, :tokens].astype(BF16)
     for j in range(probs_ref.shape[0]):
-        part = slice((2 + j) * tokens, (3 + j) * tokens)
-        probs_ref[j : j + 1, :] = out[line : line + 1, part].astype(BF16)
+        part = slice((1 + j) * tokens, (2 + j) * tokens)
+        probs_ref[j : j + 1, :] = out[feats : feats + 1, part].astype(BF16)
 
 
 def call(kernel, outs, *args, scalars=0, scratch=(), limit=32, far=0):
@@ -256,17 +261,16 @@
 
 
 def shards(tokens, cotangent, routes, gate_probs, w_gate, w_up, w_down, tile_noise):
-    nodes = lax.axis_size("node")
-    local = lax.axis_size("local")
-    chips = local // 2
+    columns = lax.axis_size("x")
+    nodes = columns * lax.axis_size("z")
+    chips = lax.axis_size("y")
     count, feats = tokens.shape
     slots = 2 * nodes
     gate, up, down, noise = w_gate[0], w_up[0], w_down[0], tile_noise[0]
     width, hid = gate.shape
     routes_t = routes.T
-    same_core = [[2 * y + c for y in range(chips)] for c in range(2)]
-    swap = [(i, i ^ 1) for i in range(local)]
-    core = lax.rem(lax.axis_index("local"), 2).astype(jnp.int32).reshape(1)
+    swap = [(0, 1), (1, 0)]
+    core = lax.axis_index("core").astype(jnp.int32).reshape(1)
 
     given = (routes_t, gate_probs.T, tokens.T, cotangent.T)
     (sent,) = call(
@@ -276,7 +280,7 @@
         scratch=[pltpu.VMEM(a.shape, a.dtype) for a in given] + [pltpu.SemaphoreType.DMA((4,))],
         far=4,
     )
-    got = lax.all_to_all(sent.reshape(nodes, 8, LANES), "node", 0, 0, tiled=True)
+    got = lax.all_to_all(sent.reshape(nodes, 8, LANES), NODE, 0, 0, tiled=True)
     later, _ = lax.optimization_barrier((core, sent))
     scaled = call(
         scale_kernel,
@@ -295,19 +299,20 @@
         [shape((2 * feats + TAIL, slots), F32), shape((8, slots), F32)],
         got.reshape(8 * nodes, LANES),
     )
-    rows = lax.all_gather(xdy.astype(F16), "local", axis=0).astype(BF16)
-    high = feats + 16
+    rows = lax.all_gather(xdy.astype(F16), LOCAL, axis=0).astype(BF16)
+    lanes = 2 * LANES
+    height = slots // columns
     keep, send, d_all = call(
         main_kernel,
         [
-            pltpu.VMEM((chips, high, slots), BF16),
-            pltpu.VMEM((chips, high, slots), BF16),
+            pltpu.VMEM((columns, chips, height, lanes), BF16),
+            pltpu.VMEM((columns, chips, height, lanes), BF16),
             pltpu.VMEM((slots, 3 * hid), BF16),
         ],
         core, prob, held(rows, pltpu.VMEM), *[held(a, pltpu.HBM) for a in (tall, eff_down)],
         scalars=1,
         scratch=[
-            pltpu.VMEM((width, 2 * hid), BF16),
+            pltpu.VMEM((width + lanes - feats, 2 * hid), BF16),
             pltpu.VMEM((hid, width), BF16),
             pltpu.VMEM((width, slots), BF16),
             pltpu.VMEM((width, slots), BF16),
@@ -315,39 +320,46 @@
         ],
         far=2,
     )
-    came = lax.ppermute(send, "local", swap)
+    came = lax.ppermute(send, "core", swap)
     pair = (keep.astype(F32) + came.astype(F32)).astype(BF16)
-    parts = lax.all_to_all(pair, "local", 0, 0, axis_index_groups=same_core, tiled=True)
+    pair = pair.reshape(columns * chips, height, lanes)
+    parts = lax.all_to_all(pair, ("x", "y"), 0, 0, tiled=True)
     (noise_grad,) = call(
         noise_kernel,
         [shape(noise.shape, F32)],
         rows, d_all, gate, up, down_t,
         scratch=[pltpu.VMEM((width, slots), BF16), pltpu.VMEM((width, slots), BF16)],
     )
-    (home,) = call(collect_kernel, [shape((4 * nodes, LANES))], parts)
+    (home,) = call(collect_kernel, [shape((slots, lanes))], parts)
     routes_later, home = lax.optimization_barrier((routes_t, home))
-    back = lax.all_to_all(home.reshape(nodes, 4, LANES), "node", 0, 0, tiled=True)
+    home = home.reshape(DEPTH, 2 * columns, lanes)
+    back = lax.all_to_all(home, "z", 0, 0, tiled=True).reshape(slots, lanes)
     top = routes.shape[1]
-    (chosen,) = call(choose_kernel, [shape((4 * nodes, (2 + top) * count))], routes_later)
+    (chosen,) = call(choose_kernel, [shape((slots, (1 + top) * count))], routes_later)
     token_t, probs_t = call(
-        finish_kernel,
-        [shape((feats, count)), shape((top, count))],
-        back.reshape(4 * nodes, LANES),
-        chosen,
+        finish_kernel, [shape((feats, count)), shape((top, count))], back, chosen
     )
     return token_t.T, probs_t.T, noise_grad[None]
 
 
 def solution(mesh):
+    nodes, local = mesh.devices.shape
+    devices = mesh.devices.reshape(nodes // DEPTH, DEPTH, local // 2, 2)
     in_specs = (
-        P("node", "local"),
-        P("node", "local"),
-        P("node", None),
-        P("node", None),
-        P("node", None, "local"),
-        P("node", None, "local"),
-        P("node", "local", None),
-        P("node", None, None, "local"),
-    )
-    out_specs = (P("node", "local"), P("node", None), P("node", None, None, "local"))
-    return jax.shard_map(shards, mesh=mesh, in_specs=in_specs, out_specs=out_specs, check_vma=False)
+        P(NODE, LOCAL),
+        P(NODE, LOCAL),
+        P(NODE, None),
+        P(NODE, None),
+        P(NODE, None, LOCAL),
+        P(NODE, None, LOCAL),
+        P(NODE, LOCAL, None),
+        P(NODE, None, None, LOCAL),
+    )
+    out_specs = (P(NODE, LOCAL), P(NODE, None), P(NODE, None, None, LOCAL))
+    return jax.shard_map(
+        shards,
+        mesh=jax.sharding.Mesh(devices, NODE + LOCAL),
+        in_specs=in_specs,
+        out_specs=out_specs,
+        check_vma=False,
+    )

time: 117 us -> 117 us (level)
  the two profiles are of different devices: /device:TPU:1 before, /device:TPU:8 now
where the time goes in v3:
time: 117 us; the launch traced here: 116 us
  blocking collectives  48.4 us (41%)
  starting transfers between devices  28.1 us (24%)
  waiting for transfers between devices  19.3 us (16%)
  Pallas kernels  11.9 us (10%)
  local copies, waits for them, and re-layouts  7.35 us (6%)
    all_to_all x1, blocking collectives, shards(): parts = lax.all_to_all(pair, ('x', 'y'), 0, 0, tiled=True)  26.1 us
    all_gather x1, blocking collectives, shards(): rows = lax.all_gather(xdy.astype(F16), LOCAL, axis=0).astype(BF16)  22.3 us
    all_to_all x1, starting transfers between devices, shards(): got = lax.all_to_all(sent.reshape(nodes, 8, LANES), NODE, 0, 0, tiled=True)  22.2 us
    pallas_call x8, Pallas kernels, call(): pl.pallas_call(kernel, out_shape=outs, in_specs=specs, out_specs=[pl.Bloc...  11.9 us
    all_to_all x1, waiting for transfers between devices, shards(): got = lax.all_to_all(sent.reshape(nodes, 8, LANES), NODE, 0, 0, tiled=True)  9.58 us
    all_to_all x1, waiting for transfers between devices, shards(): back = lax.all_to_all(home, 'z', 0, 0, tiled=True).reshape(slots, lanes)  8.22 us
    unnamed x16, local copies, waits for them, and re-layouts  7.35 us
    all_to_all x1, starting transfers between devices, shards(): back = lax.all_to_all(home, 'z', 0, 0, tiled=True).reshape(slots, lanes)  3.49 us
  transfers between devices with their start and end apart: 3, of which 3 were waited for; matrix products, arithmetic and copies ran while one was open for 1% of the time, Pallas kernels for 3%

profile of v3, /device:TPU:8, one launch (start us, length us, event | category | flops | bytes accessed | tf_op | source)
XLA Modules:
  0.0 116.3 jit_solution(390600641977730642)
XLA Ops:
  0.6 2.3 %shard_map.103 = bf16[512,128]{1,0:T(8,128)(2,1)} custom-call(s32[8,128]{1,0:T(8,128)} %bitcast.31, bf16[8,128]{1,0:T(8,128)(2,1)} %bitcast.36, bf16[224,128]{1,0:T(8,128)(2,1)} %bitcast.34, bf16[224,128]{1,0:T(8,128)(2,1)} %bitcast.35), custom_call_target="tpu_custom_call" | custom-call | bytes 251904 | tf_op jit(solution)/shard_map/pallas_call | solution.py:248
  2.9 22.2 %all-to-all-start = ((bf16[64,8,128]{2,1,0:T(8,128)(2,1)}), bf16[64,8,128]{2,1,0:T(8,128)(2,1)S(1)}, u32[]{:S(2)}, u32[]{:S(2)}) async-start(bf16[64,8,128]{2,1,0:T(8,128)(2,1)} %bitcast.5), calls=%async_computation | async-start | bytes 262144 | tf_op jit(solution)/shard_map/all_to_all | solution.py:283
  25.2 0.8 copy.14
  26.0 1.2 %copy-done = bf16[1,3584,128]{2,1,0:T(8,128)(2,1)S(1)} copy-done((bf16[1,3584,128]{2,1,0:T(8,128)(2,1)S(1)}, bf16[1,3584,128]{2,1,0:T(8,128)(2,1)}, u32[]{:S(2)}) %copy-start) | copy-done | bytes 917528
  27.1 1.2 %copy-done.2 = bf16[1,3584,128]{2,1,0:T(8,128)(2,1)S(1)} copy-done((bf16[1,3584,128]{2,1,0:T(8,128)(2,1)S(1)}, bf16[1,3584,128]{2,1,0:T(8,128)(2,1)}, u32[]{:S(2)}) %copy-start.2) | copy-done | bytes 917528
  28.3 1.2 %copy-done.5 = bf16[1,128,3584]{2,1,0:T(8,128)(2,1)S(1)} copy-done((bf16[1,128,3584]{2,1,0:T(8,128)(2,1)S(1)}, bf16[1,128,3584]{2,1,0:T(8,128)(2,1)}, u32[]{:S(2)}) %copy-start.5) | copy-done | bytes 917528
  29.5 2.4 %shard_map.104 = (bf16[3584,256]{1,0:T(8,128)(2,1)}, bf16[128,3584]{1,0:T(8,128)(2,1)}, bf16[3584,128]{1,0:T(8,128)(2,1)}) custom-call(s32[1]{0:T(128)} %bitcast.1.after_ref.core_ref, bf16[3584,128]{1,0:T(8,128)(2,1)S(1)} %bitcast.22, bf16[3584,128]{1,0:T(8,128)(2,1)S(1)} %bitcast.24, bf16[128,3584]{1,0:T(8,128)(2,1)S(1)} %bitcast.26, f32[3,28,128]{2,1,0:T(8,128)S(1)} %bitcast.30), custom_call_target="tpu_custom_call" | custom-call | bytes 6465540 | tf_op jit(solution)/shard_map/pallas_call | solution.py:248
  31.9 9.6 %all-to-all-done = bf16[64,8,128]{2,1,0:T(8,128)(2,1)S(1)} async-done(((bf16[64,8,128]{2,1,0:T(8,128)(2,1)}), bf16[64,8,128]{2,1,0:T(8,128)(2,1)S(1)}, u32[]{:S(2)}, u32[]{:S(2)}) %all-to-all-start) | async-done | bytes 131104 | tf_op jit(solution)/shard_map/all_to_all | solution.py:283
  41.5 0.4 shard_map.105
  41.9 22.3 %all-gather.2 = f16[7424,128]{1,0:T(8,128)(2,1)S(1)} all-gather(f16[464,128]{1,0:T(8,128)(2,1)S(1)} %convert_element_type.15), channel_id=2, replica_groups=mesh['x'=4,'z'=16,'y'=8,'core'=2] {'y','core'}, dimensions={0}, use_global_device_ids=true | all-gather | bytes 2019328 | tf_op jit(solution)/shard_map/all_gather | solution.py:302
  64.2 0.2 convert_element_type.20
  64.4 3.6 %shard_map.106 = (bf16[4,8,32,256]{3,2,1,0:T(8,128)(2,1)S(1)}, bf16[4,8,32,256]{3,2,1,0:T(8,128)(2,1)S(1)}, bf16[128,384]{1,0:T(8,128)(2,1)S(1)}) custom-call(s32[1]{0:T(128)} %bitcast.1.after_ref.core_ref, f32[8,128]{1,0:T(8,128)S(1)} %get-tuple-element.25.prob_ref, bf16[16,464,128]{2,1,0:T(8,128)(2,1)S(1)} %bitcast.20, ...), custom_call_target="tpu_custom_call" | custom-call | bytes 5804036 | tf_op jit(solution)/shard_map/pallas_call | solution.py:248
  68.0 2.4 %collective-permute-start = (bf16[4,8,32,256]{3,2,1,0:T(8,128)(2,1)S(1)}, bf16[4,8,32,256]{3,2,1,0:T(8,128)(2,1)S(1)}, u32[]{:S(2)}, u32[]{:S(2)}) collective-permute-start(bf16[4,8,32,256]{3,2,1,0:T(8,128)(2,1)S(1)} %get-tuple-element.30), channel_id=1, source_target_pairs={{0,1},{1,0},{2,3},{3,2},{4,5},{5,4},{6,7},{7,6},{8,9},{9,8},{10,11... | collective-permute-start | bytes 1572872 | tf_op jit(solution)/shard_map/ppermute | solution.py:323
  70.4 1.5 %collective-permute-done = bf16[4,8,32,256]{3,2,1,0:T(8,128)(2,1)S(1)} collective-permute-done((bf16[4,8,32,256]{3,2,1,0:T(8,128)(2,1)S(1)}, bf16[4,8,32,256]{3,2,1,0:T(8,128)(2,1)S(1)}, u32[]{:S(2)}, u32[]{:S(2)}) %collective-permute-start) | collective-permute-done | bytes 524320 | tf_op jit(solution)/shard_map/ppermute | solution.py:323
  72.2 26.1 %all_to_all.15.parts_ref = bf16[32,32,256]{2,1,0:T(8,128)(2,1)S(1)} all-to-all(bf16[32,32,256]{2,1,0:T(8,128)(2,1)S(1)} %bitcast.33), channel_id=1, replica_groups=mesh['x'=4,'z'=16,'y'=8,'core'=2] {'x','y'}, dimensions={0} | all-to-all | bytes 1048576 | tf_op jit(solution)/shard_map/all_to_all | solution.py:326
  98.3 0.8 shard_map.107
  99.1 3.5 %all-to-all-start.2 = ((bf16[16,8,256]{2,1,0:T(8,128)(2,1)}), bf16[16,8,256]{2,1,0:T(8,128)(2,1)S(1)}, u32[]{:S(2)}, u32[]{:S(2)}) async-start(bf16[16,8,256]{2,1,0:T(8,128)(2,1)} %bitcast.12), calls=%async_computation.2 | async-start | bytes 131072 | tf_op jit(solution)/shard_map/all_to_all | solution.py:336
  102.7 1.2 %copy-done.3 = bf16[1,3584,128]{2,1,0:T(8,128)(2,1)S(1)} copy-done((bf16[1,3584,128]{2,1,0:T(8,128)(2,1)S(1)}, bf16[1,3584,128]{2,1,0:T(8,128)(2,1)}, u32[]{:S(2)}) %copy-start.3) | copy-done | bytes 917528
  103.8 1.2 %copy-done.4 = bf16[3584,128]{1,0:T(8,128)(2,1)S(1)} copy-done((bf16[3584,128]{1,0:T(8,128)(2,1)S(1)}, bf16[3584,128]{1,0:T(8,128)(2,1)}, u32[]{:S(2)}) %copy-start.4) | copy-done | bytes 917528
  105.0 1.2 %shard_map.110 = f32[3,28,128]{2,1,0:T(8,128)S(1)} custom-call(bf16[16,464,128]{2,1,0:T(8,128)(2,1)S(1)} %bitcast.21, bf16[128,384]{1,0:T(8,128)(2,1)S(1)} %get-tuple-element.35.d_ref, bf16[3584,128]{1,0:T(8,128)(2,1)S(1)} %bitcast.23, bf16[3584,128]{1,0:T(8,128)(2,1)S(1)} %bitcast.25, bf16[3584,128]{1,0:T(8,128)(2,1)S(1)} %copy-done.4), custom_call_target="tpu_custom_call" | custom-call | bytes 4794368 | tf_op jit(solution)/shard_map/pallas_call | solution.py:248
  106.2 0.7 copy.11
  106.9 0.2 shard_map.108.chosen_ref
  107.1 8.2 %all-to-all-done.2 = bf16[16,8,256]{2,1,0:T(8,128)(2,1)S(1)} async-done(((bf16[16,8,256]{2,1,0:T(8,128)(2,1)}), bf16[16,8,256]{2,1,0:T(8,128)(2,1)S(1)}, u32[]{:S(2)}, u32[]{:S(2)}) %all-to-all-start.2) | async-done | bytes 65568 | tf_op jit(solution)/shard_map/all_to_all | solution.py:336
  115.3 0.9 shard_map.109
  (11 shorter events, 0.2 us)
Async XLA Ops:
  2.9 38.6 %all-to-all-start = ((bf16[64,8,128]{2,1,0:T(8,128)(2,1)}), bf16[64,8,128]{2,1,0:T(8,128)(2,1)S(1)}, u32[]{:S(2)}, u32[]{:S(2)}) async-start(bf16[64,8,128]{2,1,0:T(8,128)(2,1)} %bitcast.5), calls=%async_computation | async-start | bytes 262144 | tf_op jit(solution)/shard_map/all_to_all | solution.py:283
  26.0 1.2 %copy-start = (bf16[1,3584,128]{2,1,0:T(8,128)(2,1)S(1)}, bf16[1,3584,128]{2,1,0:T(8,128)(2,1)}, u32[]{:S(2)}) copy-start(bf16[1,3584,128]{2,1,0:T(8,128)(2,1)} %param.12) | copy-start | bytes 2752516
  27.1 1.2 %copy-start.2 = (bf16[1,3584,128]{2,1,0:T(8,128)(2,1)S(1)}, bf16[1,3584,128]{2,1,0:T(8,128)(2,1)}, u32[]{:S(2)}) copy-start(bf16[1,3584,128]{2,1,0:T(8,128)(2,1)} %param.13) | copy-start | bytes 2752516
  28.3 1.2 %copy-start.5 = (bf16[1,128,3584]{2,1,0:T(8,128)(2,1)S(1)}, bf16[1,128,3584]{2,1,0:T(8,128)(2,1)}, u32[]{:S(2)}) copy-start(bf16[1,128,3584]{2,1,0:T(8,128)(2,1)} %param.14) | copy-start | bytes 2752516
  68.0 34.6 %copy-start.1 = (bf16[1,3584,128]{2,1,0:T(8,128)(2,1)S(1)}, bf16[1,3584,128]{2,1,0:T(8,128)(2,1)}, u32[]{:S(2)}) copy-start(bf16[1,3584,128]{2,1,0:T(8,128)(2,1)} %param.12) | copy-start | bytes 2752516
  68.0 3.9 %collective-permute-start = (bf16[4,8,32,256]{3,2,1,0:T(8,128)(2,1)S(1)}, bf16[4,8,32,256]{3,2,1,0:T(8,128)(2,1)S(1)}, u32[]{:S(2)}, u32[]{:S(2)}) collective-permute-start(bf16[4,8,32,256]{3,2,1,0:T(8,128)(2,1)S(1)} %get-tuple-element.30), channel_id=1, source_target_pairs={{0,1},{1,0},{2,3},{3,2},{4,5},{5,4},{6,7},{7,6},{8,9},{9,8},{10,11... | collective-permute-start | bytes 1572872 | tf_op jit(solution)/shard_map/ppermute | solution.py:323
  99.1 16.2 %all-to-all-start.2 = ((bf16[16,8,256]{2,1,0:T(8,128)(2,1)}), bf16[16,8,256]{2,1,0:T(8,128)(2,1)S(1)}, u32[]{:S(2)}, u32[]{:S(2)}) async-start(bf16[16,8,256]{2,1,0:T(8,128)(2,1)} %bitcast.12), calls=%async_computation.2 | async-start | bytes 131072 | tf_op jit(solution)/shard_map/all_to_all | solution.py:336
  102.6 1.2 %copy-start.3 = (bf16[1,3584,128]{2,1,0:T(8,128)(2,1)S(1)}, bf16[1,3584,128]{2,1,0:T(8,128)(2,1)}, u32[]{:S(2)}) copy-start(bf16[1,3584,128]{2,1,0:T(8,128)(2,1)} %param.13) | copy-start | bytes 2752516
  103.8 1.2 %copy-start.4 = (bf16[3584,128]{1,0:T(8,128)(2,1)S(1)}, bf16[3584,128]{1,0:T(8,128)(2,1)}, u32[]{:S(2)}) copy-start(bf16[3584,128]{1,0:T(8,128)(2,1)} %get-tuple-element.36.down_t_ref) | copy-start | bytes 2752516
  105.0 1.9 %copy-start.6 = (s32[128,8]{0,1:T(8,128)S(1)}, s32[128,8]{0,1:T(8,128)}, u32[]{:S(2)}) copy-start(s32[128,8]{0,1:T(8,128)} %param.10) | copy-start | bytes 12292
